TPU v7x, 32 devices: a whole 2x2x4 slice. The times are simulated.
32 devices in a mesh: clique: 4 (over y, x), copy: 8 (over z, core).
Axes of the slice: x: 2, y: 2, z: 4, core: 2. Of those that a mesh axis runs over, the one named last changes fastest.
Arguments:
- out_grad: bfloat16 [65536, 512], P(('clique', 'copy')), may hold values from -6 to 6
- pre_act: bfloat16 [65536, 512], P(('clique', 'copy')), may hold values from -6 to 6
- batch_count: int32 [32], P(('clique', 'copy')), may hold values from 1024 to 2048, as said below
- layer_two: bfloat16 [512, 512], replicated, may hold values from -0.25 to 0.25
- hot_slots: int32 [65536, 10], P(('clique', 'copy')), may hold values from 0 to 2047
- cold_index: int32 [65536, 15], P(('clique', 'copy')), may hold values from 0 to 2047
- hot_feats: bfloat16 [2048, 768], P('clique'), may hold values from -6 to 6
- cold_feats: bfloat16 [65536, 768], P(('clique', 'copy')), may hold values from -6 to 6
Outputs:
- grad_one: float32 [768, 512], replicated
- grad_two: float32 [512, 512], replicated
Inputs may be any that keep to these rules, and one draw needn't show every extreme that they name: `batch_count`: some device has all 2048 rows live in every draw.
All inputs are finite; a program needn't handle non-finite values.
Results may differ from a plain program's by a relative error of at most 0.015.
Values may be sent and summed in bfloat16 or wider, within the bound.
No kernel may reach another device: no remote copies, remote signals or barrier semaphores. Data moves between devices by JAX's collectives and lax.ppermute only.
A program may use at most 128 MiB of HBM per device.

v0:
```python
import functools

import jax
import jax.numpy as jnp
from jax import lax
from jax.experimental import pallas as pl
from jax.experimental.pallas import tpu as pltpu
from jax.sharding import PartitionSpec as P

F32 = jnp.float32
BF16 = jnp.bfloat16
I16 = jnp.int16
FIELDS = 4
TILE = 16
HALF_MIB = 16
ROWS_MIB = 32


def whole():
    return pl.BlockSpec(memory_space=pltpu.VMEM)


def scalars():
    return pl.BlockSpec(memory_space=pltpu.SMEM)


def in_place():
    return pl.BlockSpec(memory_space=pl.ANY)


def params(mebibytes):
    return pltpu.CompilerParams(vmem_limit_bytes=mebibytes << 20)


def cost(flops, moved):
    return pl.CostEstimate(flops=int(flops), bytes_accessed=int(moved), transcendentals=0)


def transposed_dot(left, right):
    return lax.dot_general(left, right, (((0,), (0,)), ((), ())), preferred_element_type=F32)


def half_kernel(place_ref, feats_ref, half_ref):
    rows = half_ref.shape[0]
    here = pl.ds(pl.multiple_of(place_ref[1] * rows, TILE), rows)
    half_ref[...] = feats_ref[here, :]


def half_of(place, feats):
    rows, d_in = feats.shape
    return pl.pallas_call(
        half_kernel,
        in_specs=[scalars(), whole()],
        out_specs=whole(),
        out_shape=jax.ShapeDtypeStruct((rows // 2, d_in), BF16),
        compiler_params=params(HALF_MIB),
        cost_estimate=cost(10**10, 10**8),
        name="half_of",
    )(place, feats)


def halves(total_ref, own_ref, send_ref, own_shard, own_core, members):
    wide = own_ref.shape[1]
    mine = pl.ds(pl.multiple_of(own_core * wide, wide), wide)
    twin = pl.ds(pl.multiple_of((1 - own_core) * wide, wide), wide)
    rows = own_ref.shape[0] // members
    for member in range(members):
        here = slice(member * rows, (member + 1) * rows)
        there = pl.ds(pl.multiple_of((member ^ own_shard) * rows, TILE), rows)
        own_ref[there, :] = total_ref[here, mine].astype(BF16)
        send_ref[there, :] = total_ref[here, twin].astype(BF16)


def build_words(index, q_rows, store):
    terms = index.shape[0]
    shift = q_rows.bit_length() - 1
    low = index & (q_rows - 1)
    one = jnp.left_shift(jnp.ones_like(index), (index >> shift) * 4)
    unit = one
    for other in range(1, terms):
        turned_low = jnp.concatenate([low[other:], low[:other]], axis=0)
        turned = jnp.concatenate([one[other:], one[:other]], axis=0)
        unit = unit + jnp.where(turned_low == low, turned, jnp.zeros_like(turned))
    tall = min(256, q_rows) // TILE
    shape = (tall, TILE, 128)
    place = lax.broadcasted_iota(jnp.int32, shape, 0) * TILE + lax.broadcasted_iota(jnp.int32, shape, 1)
    place = place.astype(I16)

    def tile(row):
        return jnp.broadcast_to(row, (TILE, 128)).astype(I16)[None]

    lows = [tile(low[k : k + 1, :]) for k in range(terms)]
    units = [tile(unit[k : k + 1, :]) for k in range(terms)]
    for top in range(0, q_rows // TILE, tall):
        word = jnp.zeros(shape, I16)
        for k in range(terms):
            word = jnp.where(place == lows[k] - I16(top * TILE), units[k], word)
        store(top, tall, word)


def unpack(word_ref, field, count_ref, part=0, parts=1):
    deep = word_ref.shape[0] // parts
    words = word_ref[part * deep : (part + 1) * deep, :, :]
    if field < FIELDS - 1:
        counts = words & (15 << (4 * field))
    else:
        counts = (words >> (4 * field)) & 15
    rows = deep * TILE
    count_ref[part * rows : (part + 1) * rows, :] = counts.astype(BF16).reshape(rows, count_ref.shape[1])


def unpacked_scale(field):
    return 16.0**field if field < FIELDS - 1 else 1.0


def rows_kernel(
    shard_bits, half_rows, chunks, members,
    place_ref, count_ref, index_in, out_grad_ref, pre_act_in, layer_two_in,
    row_grad_out, own_ref, send_ref, word_out,
    index_ref, masked_ref, pre_act_ref, layer_two_ref, row_grad_ref, word_ref, sum_ref,
):
    index_ref[...] = index_in[...]
    pre_act_ref[...] = pre_act_in[...]
    layer_two_ref[...] = layer_two_in[...]
    rows = out_grad_ref.shape[0] // chunks
    blocks = [slice(chunk * rows, (chunk + 1) * rows) for chunk in range(chunks)]
    own_shard, own_core = place_ref[0], place_ref[1]
    part_bits = shard_bits - 1

    def build(tile):
        lanes = slice(tile * 128, (tile + 1) * 128)
        index = index_ref[:, lanes]
        row = index & ((1 << part_bits) - 1)
        half = ((index >> part_bits) & 1) ^ own_core ^ 1
        index = half * half_rows + (((index >> shard_bits) ^ own_shard) << part_bits) + row

        def store(top, tall, words):
            word_ref[top : top + tall, :, lanes] = words

        build_words(index, word_ref.shape[0] * TILE, store)

    tiles = row_grad_ref.shape[0] // 128
    ends = [tiles * chunk // chunks for chunk in range(chunks + 1)]
    for chunk, block in enumerate(blocks):
        live = count_ref[0] - chunk * rows

        @pl.when(live >= rows)
        def _(block=block):
            masked_ref[block, :] = out_grad_ref[block, :]

        @pl.when(live < rows)
        def _(block=block, live=live):
            out_grad = out_grad_ref[block, :].astype(F32)
            place = lax.broadcasted_iota(jnp.int32, out_grad.shape, 0)
            masked = jnp.where(place < live, out_grad, jnp.zeros_like(out_grad))
            masked_ref[block, :] = masked.astype(BF16)

    for chunk, block in enumerate(blocks):
        masked = masked_ref[block, :]
        pre_act = pre_act_ref[block, :]
        back = lax.dot_general(
            masked, layer_two_ref[...], (((1,), (1,)), ((), ())), preferred_element_type=F32
        )
        row_grad_ref[block, :] = jnp.where(
            pre_act.astype(F32) > 0, back, jnp.zeros_like(back)
        ).astype(BF16)
        activ = jnp.maximum(pre_act, jnp.zeros_like(pre_act))
        part = transposed_dot(activ, masked)
        sum_ref[...] = part if chunk == 0 else sum_ref[...] + part
        for tile in range(ends[chunk], ends[chunk + 1]):
            build(tile)
    row_grad_out[...] = row_grad_ref[...]
    word_out[...] = word_ref[...]
    halves(sum_ref, own_ref, send_ref, own_shard, own_core, members)


def row_gradients(place, batch_count, out_grad, pre_act, layer_two, index, hot_total, shard_rows):
    rows, d_out = out_grad.shape
    d_h = pre_act.shape[1]
    chunks = 4
    deep = hot_total // FIELDS // TILE
    half = jax.ShapeDtypeStruct((d_h, d_out // 2), BF16)
    return pl.pallas_call(
        functools.partial(
            rows_kernel,
            shard_rows.bit_length() - 1,
            hot_total // 2,
            chunks,
            hot_total // shard_rows,
        ),
        in_specs=[scalars(), scalars()] + [whole()] * 4,
        out_specs=[whole()] * 4,
        out_shape=[
            jax.ShapeDtypeStruct((rows, d_h), BF16),
            half,
            half,
            jax.ShapeDtypeStruct((deep, TILE, rows), I16),
        ],
        scratch_shapes=[
            pltpu.VMEM(index.shape, jnp.int32),
            pltpu.VMEM((rows, d_out), BF16),
            pltpu.VMEM((rows, d_h), BF16),
            pltpu.VMEM((d_h, d_out), BF16),
            pltpu.VMEM((rows, d_h), BF16),
            pltpu.VMEM((deep, TILE, rows), I16),
            pltpu.VMEM((d_h, d_out), F32),
        ],
        compiler_params=params(ROWS_MIB),
        cost_estimate=cost(10**10, 10**8),
        name="row_gradients",
    )(place, batch_count, index, out_grad, pre_act, layer_two)


def sums_of_field(counts, row_grad_ref, field, scale, out_ref, top, beside):
    tall = counts[0].shape[0]
    wide = row_grad_ref.shape[1] // 2
    for half in range(2):
        lanes = slice(half * wide, (half + 1) * wide)
        found = jnp.dot(
            counts[field % 2][...], row_grad_ref[:, lanes], preferred_element_type=F32
        )
        found = found * (scale / unpacked_scale(field))
        out_ref[top : top + tall, lanes] = found.astype(BF16)
        beside(half)


def hot_kernel(
    scale, word_in, row_grad_in, index_in, send_ref, keep_ref, cold_word_out,
    word_ref, row_grad_ref, index_ref, sums_ref, cold_word_ref, *counts
):
    word_ref[...] = word_in[...]
    row_grad_ref[...] = row_grad_in[...]
    index_ref[...] = index_in[...]
    tall, rows = counts[0].shape
    tiles = rows // 128 // FIELDS // 2
    unpack(word_ref, 0, counts[0])
    for field in range(FIELDS):

        def beside(half, field=field):
            if field + 1 < FIELDS:
                unpack(word_ref, field + 1, counts[(field + 1) % 2], half, 2)
            first = (2 * field + half) * tiles
            for tile in range(first, first + tiles):
                lanes = slice(tile * 128, (tile + 1) * 128)

                def store(top, deep, words, lanes=lanes):
                    cold_word_ref[top : top + deep, :, lanes] = words

                build_words(index_ref[:, lanes], cold_word_ref.shape[0] * TILE, store)

        sums_of_field(counts, row_grad_ref, field, scale, sums_ref, field * tall, beside)
    send_ref[...] = sums_ref[: 2 * tall, :]
    keep_ref[...] = sums_ref[2 * tall :, :]
    cold_word_out[...] = cold_word_ref[...]


def hot_sums(words, row_grad, cold_index, cold_rows, fanout):
    rows, d_h = row_grad.shape
    q_rows = words.shape[0] * TILE
    half = jax.ShapeDtypeStruct((q_rows * FIELDS // 2, d_h), BF16)
    return pl.pallas_call(
        functools.partial(hot_kernel, 1.0 / fanout),
        in_specs=[whole(), whole(), whole()],
        out_specs=[whole()] * 3,
        out_shape=[
            half,
            half,
            jax.ShapeDtypeStruct((cold_rows // FIELDS // TILE, TILE, rows), I16),
        ],
        scratch_shapes=[
            pltpu.VMEM(words.shape, I16),
            pltpu.VMEM(row_grad.shape, BF16),
            pltpu.VMEM(cold_index.shape, jnp.int32),
            pltpu.VMEM((q_rows * FIELDS, d_h), BF16),
            pltpu.VMEM((cold_rows // FIELDS // TILE, TILE, rows), I16),
            pltpu.VMEM((q_rows, rows), BF16),
            pltpu.VMEM((q_rows, rows), BF16),
        ],
        compiler_params=params(40),
        cost_estimate=cost(10**10, 10**8),
        name="hot_sums",
    )(words, row_grad, cold_index)


def cold_kernel(
    scale, word_in, row_grad_in, feats_ref, grad_out,
    word_ref, row_grad_ref, grad_ref, sums_ref, held_ref, sem, *counts
):
    fetch = pltpu.make_async_copy(feats_ref, held_ref, sem)
    fetch.start()
    word_ref[...] = word_in[...]
    row_grad_ref[...] = row_grad_in[...]
    tall = counts[0].shape[0]
    wide = held_ref.shape[1] // 2

    def add_product(field, half):
        rows, lanes = slice(field * tall, (field + 1) * tall), slice(half * wide, (half + 1) * wide)
        part = transposed_dot(held_ref[rows, lanes], sums_ref[rows, :])
        grad_ref[lanes, :] = part if field == 0 else grad_ref[lanes, :] + part

    unpack(word_ref, 0, counts[0])
    for field in range(FIELDS):
        if field == 1:
            fetch.wait()

        def beside(half, field=field):
            if field + 1 < FIELDS:
                unpack(word_ref, field + 1, counts[(field + 1) % 2], half, 2)
            if field > 0:
                add_product(field - 1, half)

        sums_of_field(counts, row_grad_ref, field, scale, sums_ref, field * tall, beside)
    for half in range(2):
        add_product(FIELDS - 1, half)
    grad_out[...] = grad_ref[...]


def cold_grad(words, row_grad, feats, fanout):
    rows, d_h = row_grad.shape
    cold_rows, d_in = feats.shape
    q_rows = cold_rows // FIELDS
    return pl.pallas_call(
        functools.partial(cold_kernel, 1.0 / fanout),
        in_specs=[whole(), whole(), in_place()],
        out_specs=whole(),
        out_shape=jax.ShapeDtypeStruct((d_in, d_h), F32),
        scratch_shapes=[
            pltpu.VMEM(words.shape, I16),
            pltpu.VMEM(row_grad.shape, BF16),
            pltpu.VMEM((d_in, d_h), F32),
            pltpu.VMEM((cold_rows, d_h), BF16),
            pltpu.VMEM((cold_rows, d_in), BF16),
            pltpu.SemaphoreType.DMA,
            pltpu.VMEM((q_rows, rows), BF16),
            pltpu.VMEM((q_rows, rows), BF16),
        ],
        compiler_params=params(40),
        cost_estimate=cost(10**10, 10**8),
        name="cold_grad",
    )(words, row_grad, feats)


def join_kernel(parts, place_ref, cold_ref, keep_ref, other_ref, *rest):
    feats, (own_ref, send_ref, sums_ref, held_ref, total_ref) = rest[:parts], rest[parts:]
    d_in, wide = own_ref.shape
    sums = keep_ref[...].astype(F32) + other_ref[...].astype(F32)
    sums_ref[...] = sums.astype(BF16)
    base = 0
    for part in feats:
        held_ref[base : base + part.shape[0], :] = part[:, :d_in]
        base += part.shape[0]
    total_ref[...] = cold_ref[...]
    for left in range(0, d_in, 256):
        rows = slice(left, left + 256)
        total_ref[rows, :] += transposed_dot(held_ref[:, rows], sums_ref[...])
    total = total_ref[...].astype(BF16)
    store_halves(total, slice(None), place_ref[1], own_ref, send_ref)


def store_halves(total, rows, own_core, own_ref, send_ref):
    wide = own_ref.shape[1]
    first, second = total[:, :wide], total[:, wide:]

    @pl.when(own_core == 0)
    def _():
        own_ref[rows, :] = first
        send_ref[rows, :] = second

    @pl.when(own_core == 1)
    def _():
        own_ref[rows, :] = second
        send_ref[rows, :] = first


def join(place, cold, keep, other, feats):
    d_in, d_h = cold.shape
    half = jax.ShapeDtypeStruct((d_in, d_h // 2), BF16)
    return pl.pallas_call(
        functools.partial(join_kernel, len(feats)),
        in_specs=[scalars()] + [whole()] * (3 + len(feats)),
        out_specs=[whole()] * 2,
        out_shape=[half, half],
        scratch_shapes=[
            pltpu.VMEM(keep.shape, BF16),
            pltpu.VMEM((keep.shape[0], d_in), BF16),
            pltpu.VMEM((d_in, d_h), F32),
        ],
        compiler_params=params(32),
        cost_estimate=cost(2 * keep.shape[0] * d_h * d_in, 4 * d_in * d_h),
        name="join",
    )(place, cold, keep, other, *feats)


def share_rows(rows, members, place_ref, core, turn):
    size = rows // members
    partner = turn
    if members == 4 and turn == 1:
        partner = 3
    elif members == 4 and turn > 1:
        partner = jnp.where(core == 0, turn - 1, 4 - turn)
    return pl.ds(pl.multiple_of((place_ref[0] ^ partner) * size, TILE), size)


def pair_kernel(place_ref, one_ref, other_ref, *out_refs):
    members = len(out_refs)
    for k, out_ref in enumerate(out_refs):
        here = share_rows(one_ref.shape[0], members, place_ref, place_ref[1], k)
        total = one_ref[here, :].astype(F32) + other_ref[here, :].astype(F32)
        out_ref[...] = total.astype(BF16)


def pair_sums(place, one, other, members):
    rows, wide = one.shape
    share = jax.ShapeDtypeStruct((rows // members, wide), BF16)
    return pl.pallas_call(
        pair_kernel,
        in_specs=[scalars()] + [whole()] * 2,
        out_specs=[whole()] * members,
        out_shape=[share] * members,
        compiler_params=params(16),
        cost_estimate=cost(0, 6 * rows * wide),
        name="pair_sums",
    )(place, one, other)


def laid_turns(members):
    return [0, members - 1, *range(1, members - 1)]


def lay_kernel(members, parts, twin, place_ref, *refs):
    halves_in, refs = refs[:parts], refs[parts:]
    refs = refs[2:] if twin else refs
    outs, held, sems = refs[:2], refs[2:4], refs[4]
    core = 1 - place_ref[1] if twin else place_ref[1]
    wide = halves_in[0].shape[1]
    lanes = pl.ds(pl.multiple_of(core * wide, wide), wide)
    each = members // parts
    copies = []
    for k, turn in enumerate(laid_turns(members)):
        base = k % each * (halves_in[0].shape[0] // each)
        for at, (out_ref, held_ref) in enumerate(zip(outs, held)):
            here = share_rows(out_ref.shape[0], members, place_ref, core, turn)
            held_ref[here, :] = halves_in[k // each][base : base + here.size, :].astype(F32)
            copy = pltpu.make_async_copy(
                held_ref.at[here, :], out_ref.at[here, lanes], sems.at[2 * k + at]
            )
            copy.start()
            copies.append(copy)
            base += here.size
    for copy in copies:
        copy.wait()


def lay(place, parts, members, rows_of, before=()):
    wide = parts[0].shape[1]
    count = 1 + len(parts)
    return pl.pallas_call(
        functools.partial(lay_kernel, members, len(parts), bool(before)),
        in_specs=[scalars()] + [whole()] * len(parts) + [in_place()] * len(before),
        out_specs=[in_place()] * len(rows_of),
        out_shape=[jax.ShapeDtypeStruct((rows, 2 * wide), F32) for rows in rows_of],
        input_output_aliases={count + at: at for at in range(len(before))},
        scratch_shapes=[pltpu.VMEM((rows, wide), F32) for rows in rows_of]
        + [pltpu.SemaphoreType.DMA((2 * members,))],
        compiler_params=params(16),
        cost_estimate=cost(10**10, 10**8),
        name="lay",
    )(place, *parts, *before)


def exchange(array, axis, step):
    size = lax.axis_size(axis)
    return lax.ppermute(array, axis, [(source, source ^ step) for source in range(size)])


def added(*arrays):
    total = arrays[0].astype(F32)
    for array in arrays[1:]:
        total = total + array.astype(F32)
    return total.astype(BF16)


def route_of(n_clique, n_copy, turn):
    moves = [(0, 0), (3, 3), (1, 2), (2, 1)][turn] if n_clique == 4 else (turn, turn)
    return [
        (i * n_copy + j, (i ^ moves[j & 1]) * n_copy + j)
        for i in range(n_clique)
        for j in range(n_copy)
    ]


def trade(arrays):
    n_clique, n_copy = lax.axis_size("clique"), lax.axis_size("copy")
    return [arrays[0]] + [
        lax.ppermute(arrays[turn], ("clique", "copy"), route_of(n_clique, n_copy, turn))
        for turn in range(1, n_clique)
    ]


def sum_over_slice(shares, two):
    own = jnp.concatenate([added(*trade(shares)), two], axis=0)
    n_copy = lax.axis_size("copy")
    steps = [2 << bit for bit in range((n_copy // 2).bit_length() - 1)]
    for near, far in zip(steps, reversed(steps)):
        route = [(j, j ^ (far if j & 1 else near)) for j in range(n_copy)]
        own = added(own, lax.ppermute(own, "copy", route))
    return trade([own] * len(shares))


def gather(own, two):
    members = lax.axis_size("clique")
    rows = two.shape[0] // members
    shares = [two[k * rows : (k + 1) * rows] for k in range(members)]
    middle, d_in = own.shape[0] // 2, own.shape[1]
    if members != 4 or rows != middle:
        feats = [own] + [exchange(own, "clique", k) for k in range(1, members)]
        got = shares[:1] + [exchange(shares[k], "clique", k) for k in range(1, members)]
        return feats, added(*got)
    one, other = exchange(own, "clique", 1), exchange(own, "clique", 2)
    top = exchange(jnp.concatenate([other[:middle], shares[1]], axis=1), "clique", 1)
    bottom = exchange(jnp.concatenate([one[middle:], shares[2]], axis=1), "clique", 2)
    far = exchange(shares[3], "clique", 3)
    total = added(shares[0], top[:, d_in:], bottom[:, d_in:], far)
    return [own, one, other, top, bottom], total


def on_device(
    out_grad, pre_act, batch_count, layer_two, hot_slots, cold_index, hot_feats, cold_feats
):
    n_clique = lax.axis_size("clique")
    shard_rows, d_in = hot_feats.shape
    d_h = pre_act.shape[1]
    cold_rows = cold_feats.shape[0]
    fanout = hot_slots.shape[1] + cold_index.shape[1]
    copy_at = lax.axis_index("copy")
    place = jnp.stack([lax.axis_index("clique"), copy_at & 1]).astype(jnp.int32)

    half_feats = half_of(place, hot_feats)
    row_grad, own_two, twin_two, words = row_gradients(
        place, batch_count, out_grad, pre_act, layer_two, hot_slots.T, shard_rows * n_clique, shard_rows
    )
    two = added(own_two, exchange(twin_two, "copy", 1))
    feats, two = gather(half_feats, two)
    send, keep, words = hot_sums(words, row_grad, cold_index.T, cold_rows, fanout)
    other = exchange(send, "copy", 1)
    cold = cold_grad(words, row_grad, cold_feats, fanout)
    own_one, twin_one = join(place, cold, keep, other, feats)
    shares = pair_sums(place, own_one, exchange(twin_one, "copy", 1), n_clique)
    shares = sum_over_slice(shares, two)
    middle = n_clique // 2
    shares = [shares[turn] for turn in laid_turns(n_clique)]
    parts = [jnp.concatenate(part, axis=0) for part in (shares[:middle], shares[middle:])]
    others = [exchange(part, "copy", 1) for part in parts]
    rows_of = (d_in, d_h)
    own = lay(place, parts, n_clique, rows_of)
    return tuple(lay(place, others, n_clique, rows_of, own))


def solution(mesh):
    placed = (
        P(("clique", "copy"), None),
        P(("clique", "copy"), None),
        P(("clique", "copy")),
        P(),
        P(("clique", "copy"), None),
        P(("clique", "copy"), None),
        P("clique", None),
        P(("clique", "copy"), None),
    )
    return jax.shard_map(
        on_device, mesh=mesh, in_specs=placed, out_specs=(P(), P()), check_vma=False
    )
```

profile of v0, /device:TPU:0, one launch (start us, length us, event | category | flops | bytes accessed | tf_op | source)
XLA Modules:
  0.0 68.8 jit_solution(11697781728231976769)
XLA Ops:
  0.6 0.1 pad_add_fusion.place_ref
  0.7 1.1 %copy-done.3 = bf16[512,768]{1,0:T(8,128)(2,1)S(1)} copy-done((bf16[512,768]{1,0:T(8,128)(2,1)S(1)}, bf16[512,768]{1,0:T(8,128)(2,1)}, u32[]{:S(2)}) %copy-start.3) | copy-done | bytes 786456
  1.9 0.6 half_of.1.rest_0_
  2.4 3.0 %collective-permute-start.2 = (bf16[256,768]{1,0:T(8,128)(2,1)S(1)}, bf16[256,768]{1,0:T(8,128)(2,1)S(1)}, u32[]{:S(2)}, u32[]{:S(2)}) collective-permute-start(bf16[256,768]{1,0:T(8,128)(2,1)S(1)} %half_of.1.rest_0_), channel_id=1, source_target_pairs={{0,16},{8,24},{16,0},{24,8},{1,17},{9,25},{17,1},{25,9},{2,18},{10... | collective-permute-start | bytes 1179656 | tf_op jit(solution)/shard_map/ppermute | solution.py:473
  5.5 1.5 %collective-permute-start.1 = (bf16[256,768]{1,0:T(8,128)(2,1)S(1)}, bf16[256,768]{1,0:T(8,128)(2,1)S(1)}, u32[]{:S(2)}, u32[]{:S(2)}) collective-permute-start(bf16[256,768]{1,0:T(8,128)(2,1)S(1)} %half_of.1.rest_0_), channel_id=1, source_target_pairs={{0,8},{8,0},{16,24},{24,16},{1,9},{9,1},{17,25},{25,17},{2,10},{10... | collective-permute-start | bytes 1179656 | tf_op jit(solution)/shard_map/ppermute | solution.py:473
  7.7 0.0 copy-start.6
  7.7 5.1 %row_gradients.1 = (bf16[2048,512]{1,0:T(8,128)(2,1)S(1)}, bf16[512,256]{1,0:T(8,128)(2,1)S(1)}, bf16[512,256]{1,0:T(8,128)(2,1)S(1)}, s16[32,16,2048]{2,1,0:T(8,128)(2,1)S(1)}) custom-call(s32[2]{0:T(128)S(1)} %pad_add_fusion.place_ref, s32[1]{0:T(128)S(6)} %copy.15.count_ref, s32[10,2048]{1,0:T(8,128)S(1)} %bitcast.4, bf16[2048,512]{1,0:T(8,128)(2,1)S(1)} %copy-done.1, ...), custom_call_target="tpu_custom_call" | custom-call | flops 10000000000 | bytes 100000000 | tf_op jit(solution)/shard_map/row_gradients/pallas_call | solution.py:183
  12.7 0.1 collective-permute-start.3
  12.8 0.0 copy-start
  12.8 7.4 %hot_sums.1 = (bf16[1024,512]{1,0:T(8,128)(2,1)S(1)}, bf16[1024,512]{1,0:T(8,128)(2,1)S(1)}, s16[32,16,2048]{2,1,0:T(8,128)(2,1)S(1)}) custom-call(s16[32,16,2048]{2,1,0:T(8,128)(2,1)S(1)} %get-tuple-element.17.word_in, bf16[2048,512]{1,0:T(8,128)(2,1)S(1)} %get-tuple-element.18.row_grad_in, s32[15,2048]{1,0:T(8,128)S(1)} %bitcast.5), custom_call_target="tpu_custom_call" | custom-call | flops 10000000000 | bytes 100000000 | tf_op jit(solution)/shard_map/hot_sums/pallas_call | solution.py:261
  20.2 0.5 collective-permute-start
  20.8 0.0 collective-permute-done.3
  20.8 0.1 add_convert_fusion
  20.8 0.0 collective-permute-done.2.rest_2_
  20.9 0.5 collective-permute-start.4
  21.4 0.0 collective-permute-done.1.rest_1_
  21.5 0.6 collective-permute-start.5
  22.0 6.6 %cold_grad.1.cold_ref = f32[768,512]{1,0:T(8,128)S(1)} custom-call(s16[32,16,2048]{2,1,0:T(8,128)(2,1)S(1)} %get-tuple-element.19.word_in, bf16[2048,512]{1,0:T(8,128)(2,1)S(1)} %get-tuple-element.18.row_grad_in, bf16[2048,768]{1,0:T(8,128)(2,1)S(1)} %copy-done), custom_call_target="tpu_custom_call" | custom-call | flops 10000000000 | bytes 100000000 | tf_op jit(solution)/shard_map/cold_grad/pallas_call | solution.py:322
  28.6 0.6 collective-permute-done.4.rest_3_
  29.2 0.3 collective-permute-done.5.rest_4_
  29.5 0.0 collective-permute-done.other_ref
  29.5 1.6 %join.1 = (bf16[768,256]{1,0:T(8,128)(2,1)S(1)}, bf16[768,256]{1,0:T(8,128)(2,1)S(1)}) custom-call(s32[2]{0:T(128)S(1)} %pad_add_fusion.place_ref, f32[768,512]{1,0:T(8,128)S(1)} %cold_grad.1.cold_ref, bf16[1024,512]{1,0:T(8,128)(2,1)S(1)} %get-tuple-element.20.keep_ref, bf16[1024,512]{1,0:T(8,128)(2,1)S(1)} %collective-permute-done.other_ref, ...), custom_call_target="tpu_custom_call" | custom-call | flops 805306368 | bytes 1572864 | tf_op jit(solution)/shard_map/join/pallas_call | solution.py:378
  31.2 0.1 collective-permute-start.6
  31.2 1.7 %collective-permute-start.10 = (bf16[128,256]{1,0:T(8,128)(2,1)S(1)}, bf16[128,256]{1,0:T(8,128)(2,1)S(1)}, u32[]{:S(2)}, u32[]{:S(2)}) collective-permute-start(bf16[128,256]{1,0:T(8,128)(2,1)S(1)} %get-tuple-element.33), channel_id=1, source_target_pairs={{0,24},{8,16},{16,8},{24,0},{1,25},{9,17},{17,9},{25,1},{2,26},{10... | collective-permute-start | bytes 196616 | tf_op jit(solution)/shard_map/ppermute | solution.py:473
  33.0 0.0 collective-permute-done.6.other_ref
  33.0 0.6 pair_sums.1
  33.6 1.7 %collective-permute-start.7 = (bf16[192,256]{1,0:T(8,128)(2,1)S(1)}, bf16[192,256]{1,0:T(8,128)(2,1)S(1)}, u32[]{:S(2)}, u32[]{:S(2)}) collective-permute-start(bf16[192,256]{1,0:T(8,128)(2,1)S(1)} %get-tuple-element.27), channel_id=1, source_target_pairs={{0,24},{1,25},{2,26},{3,27},{4,28},{5,29},{6,30},{7,31},{8,16},{9,... | collective-permute-start | bytes 294920 | tf_op jit(solution)/shard_map/ppermute | solution.py:495
  35.3 1.2 %collective-permute-start.8 = (bf16[192,256]{1,0:T(8,128)(2,1)S(1)}, bf16[192,256]{1,0:T(8,128)(2,1)S(1)}, u32[]{:S(2)}, u32[]{:S(2)}) collective-permute-start(bf16[192,256]{1,0:T(8,128)(2,1)S(1)} %get-tuple-element.28), channel_id=1, source_target_pairs={{0,8},{1,17},{2,10},{3,19},{4,12},{5,21},{6,14},{7,23},{8,0},{9,25... | collective-permute-start | bytes 294920 | tf_op jit(solution)/shard_map/ppermute | solution.py:495
  36.5 0.7 collective-permute-start.9
  37.2 2.7 %collective-permute-done.7 = bf16[192,256]{1,0:T(8,128)(2,1)S(1)} collective-permute-done((bf16[192,256]{1,0:T(8,128)(2,1)S(1)}, bf16[192,256]{1,0:T(8,128)(2,1)S(1)}, u32[]{:S(2)}, u32[]{:S(2)}) %collective-permute-start.7) | collective-permute-done | bytes 98336 | tf_op jit(solution)/shard_map/ppermute | solution.py:495
  40.0 1.5 %collective-permute-done.8 = bf16[192,256]{1,0:T(8,128)(2,1)S(1)} collective-permute-done((bf16[192,256]{1,0:T(8,128)(2,1)S(1)}, bf16[192,256]{1,0:T(8,128)(2,1)S(1)}, u32[]{:S(2)}, u32[]{:S(2)}) %collective-permute-start.8) | collective-permute-done | bytes 98336 | tf_op jit(solution)/shard_map/ppermute | solution.py:495
  41.5 0.1 collective-permute-done.9
  41.6 0.1 add_convert_fusion.3
  41.7 1.6 %collective-permute-start.11 = (bf16[320,256]{1,0:T(8,128)(2,1)S(1)}, bf16[320,256]{1,0:T(8,128)(2,1)S(1)}, u32[]{:S(2)}, u32[]{:S(2)}) collective-permute-start(bf16[320,256]{1,0:T(8,128)(2,1)S(1)} %pad_maximum_fusion.3), channel_id=1, source_target_pairs={{0,2},{1,5},{2,0},{3,7},{4,6},{5,1},{6,4},{7,3},{8,10},{9,13},{10,... | collective-permute-start | bytes 491528 | tf_op jit(solution)/shard_map/ppermute | solution.py:506
  43.2 4.4 %collective-permute-done.11 = bf16[320,256]{1,0:T(8,128)(2,1)S(1)} collective-permute-done((bf16[320,256]{1,0:T(8,128)(2,1)S(1)}, bf16[320,256]{1,0:T(8,128)(2,1)S(1)}, u32[]{:S(2)}, u32[]{:S(2)}) %collective-permute-start.11) | collective-permute-done | bytes 163872 | tf_op jit(solution)/shard_map/ppermute | solution.py:506
  47.6 2.8 %collective-permute-start.12 = (bf16[320,256]{1,0:T(8,128)(2,1)S(1)}, bf16[320,256]{1,0:T(8,128)(2,1)S(1)}, u32[]{:S(2)}, u32[]{:S(2)}) collective-permute-start(bf16[320,256]{1,0:T(8,128)(2,1)S(1)} %add_convert_fusion.2), channel_id=1, source_target_pairs={{0,4},{1,3},{2,6},{3,1},{4,0},{5,7},{6,2},{7,5},{8,12},{9,11},{10,... | collective-permute-start | bytes 491528 | tf_op jit(solution)/shard_map/ppermute | solution.py:506
  50.4 3.6 %collective-permute-done.12 = bf16[320,256]{1,0:T(8,128)(2,1)S(1)} collective-permute-done((bf16[320,256]{1,0:T(8,128)(2,1)S(1)}, bf16[320,256]{1,0:T(8,128)(2,1)S(1)}, u32[]{:S(2)}, u32[]{:S(2)}) %collective-permute-start.12) | collective-permute-done | bytes 163872 | tf_op jit(solution)/shard_map/ppermute | solution.py:506
  54.1 1.5 %collective-permute-start.15 = (bf16[320,256]{1,0:T(8,128)(2,1)S(1)}, bf16[320,256]{1,0:T(8,128)(2,1)S(1)}, u32[]{:S(2)}, u32[]{:S(2)}) collective-permute-start(bf16[320,256]{1,0:T(8,128)(2,1)S(1)} %add_convert_fusion.1), channel_id=1, source_target_pairs={{0,24},{1,25},{2,26},{3,27},{4,28},{5,29},{6,30},{7,31},{8,16},{9,... | collective-permute-start | bytes 491528 | tf_op jit(solution)/shard_map/ppermute | solution.py:495
  55.5 2.6 %collective-permute-start.16 = (bf16[320,256]{1,0:T(8,128)(2,1)S(1)}, bf16[320,256]{1,0:T(8,128)(2,1)S(1)}, u32[]{:S(2)}, u32[]{:S(2)}) collective-permute-start(bf16[320,256]{1,0:T(8,128)(2,1)S(1)} %add_convert_fusion.1), channel_id=1, source_target_pairs={{0,8},{1,17},{2,10},{3,19},{4,12},{5,21},{6,14},{7,23},{8,0},{9,25... | collective-permute-start | bytes 491528 | tf_op jit(solution)/shard_map/ppermute | solution.py:495
  58.2 0.0 collective-permute-start.13
  58.2 4.0 %collective-permute-done.15 = bf16[320,256]{1,0:T(8,128)(2,1)S(1)} collective-permute-done((bf16[320,256]{1,0:T(8,128)(2,1)S(1)}, bf16[320,256]{1,0:T(8,128)(2,1)S(1)}, u32[]{:S(2)}, u32[]{:S(2)}) %collective-permute-start.15) | collective-permute-done | bytes 163872 | tf_op jit(solution)/shard_map/ppermute | solution.py:495
  62.1 2.5 %collective-permute-done.16 = bf16[320,256]{1,0:T(8,128)(2,1)S(1)} collective-permute-done((bf16[320,256]{1,0:T(8,128)(2,1)S(1)}, bf16[320,256]{1,0:T(8,128)(2,1)S(1)}, u32[]{:S(2)}, u32[]{:S(2)}) %collective-permute-start.16) | collective-permute-done | bytes 163872 | tf_op jit(solution)/shard_map/ppermute | solution.py:495
  64.6 0.1 collective-permute-start.17
  64.7 0.1 collective-permute-done.13
  64.8 0.5 collective-permute-start.14
  65.3 1.7 %lay.2 = (f32[768,512]{1,0:T(8,128)}, f32[512,512]{1,0:T(8,128)}) custom-call(s32[2]{0:T(128)S(1)} %pad_add_fusion.place_ref, bf16[640,256]{1,0:T(8,128)(2,1)S(1)} %pad_maximum_fusion.refs_0_, bf16[640,256]{1,0:T(8,128)(2,1)S(1)} %constant_dynamic-update-slice_fusion.refs_1_), custom_call_target="tpu_custom_call" | custom-call | flops 10000000000 | bytes 100000000 | tf_op jit(solution)/shard_map/lay/pallas_call | solution.py:457
  67.0 0.0 collective-permute-done.17.refs_1_
  67.0 1.7 %lay.3 = (f32[768,512]{1,0:T(8,128)}, f32[512,512]{1,0:T(8,128)}) custom-call(s32[2]{0:T(128)S(1)} %pad_add_fusion.place_ref, bf16[640,256]{1,0:T(8,128)(2,1)S(1)} %collective-permute-done.14.refs_0_, bf16[640,256]{1,0:T(8,128)(2,1)S(1)} %collective-permute-done.17.refs_1_, ...), custom_call_target="tpu_custom_call", output_to_operand_aliasing={{0}: (3, {}), {1}: (4, {})} | custom-call | flops 10000000000 | bytes 100000000 | tf_op jit(solution)/shard_map/lay/pallas_call | solution.py:457
  (25 shorter events, 0.3 us)
Async XLA Ops:
  0.7 1.1 %copy-start.3 = (bf16[512,768]{1,0:T(8,128)(2,1)S(1)}, bf16[512,768]{1,0:T(8,128)(2,1)}, u32[]{:S(2)}) copy-start(bf16[512,768]{1,0:T(8,128)(2,1)} %feats_ref.3) | copy-start | bytes 2359300
  1.8 5.8 %copy-start.1 = (bf16[2048,512]{1,0:T(8,128)(2,1)S(1)}, bf16[2048,512]{1,0:T(8,128)(2,1)}, u32[]{:S(2)}) copy-start(bf16[2048,512]{1,0:T(8,128)(2,1)} %out_grad_ref.1) | copy-start | bytes 6291460
  1.8 5.8 %copy-start.2 = (bf16[2048,512]{1,0:T(8,128)(2,1)S(1)}, bf16[2048,512]{1,0:T(8,128)(2,1)}, u32[]{:S(2)}) copy-start(bf16[2048,512]{1,0:T(8,128)(2,1)} %pre_act_in.1) | copy-start | bytes 6291460
  1.8 5.8 %copy-start.4 = (bf16[512,512]{1,0:T(8,128)(2,1)S(1)}, bf16[512,512]{1,0:T(8,128)(2,1)}, u32[]{:S(2)}) copy-start(bf16[512,512]{1,0:T(8,128)(2,1)} %layer_two_in.1) | copy-start | bytes 1572868
  1.9 5.8 %copy-start.5 = (s32[2048,10]{0,1:T(8,128)S(1)}, s32[2048,10]{0,1:T(8,128)}, u32[]{:S(2)}) copy-start(s32[2048,10]{0,1:T(8,128)} %param.12) | copy-start | bytes 245764
  2.4 18.4 %collective-permute-start.2 = (bf16[256,768]{1,0:T(8,128)(2,1)S(1)}, bf16[256,768]{1,0:T(8,128)(2,1)S(1)}, u32[]{:S(2)}, u32[]{:S(2)}) collective-permute-start(bf16[256,768]{1,0:T(8,128)(2,1)S(1)} %half_of.1.rest_0_), channel_id=1, source_target_pairs={{0,16},{8,24},{16,0},{24,8},{1,17},{9,25},{17,1},{25,9},{2,18},{10... | collective-permute-start | bytes 1179656 | tf_op jit(solution)/shard_map/ppermute | solution.py:473
  5.5 16.0 %collective-permute-start.1 = (bf16[256,768]{1,0:T(8,128)(2,1)S(1)}, bf16[256,768]{1,0:T(8,128)(2,1)S(1)}, u32[]{:S(2)}, u32[]{:S(2)}) collective-permute-start(bf16[256,768]{1,0:T(8,128)(2,1)S(1)} %half_of.1.rest_0_), channel_id=1, source_target_pairs={{0,8},{8,0},{16,24},{24,16},{1,9},{9,1},{17,25},{25,17},{2,10},{10... | collective-permute-start | bytes 1179656 | tf_op jit(solution)/shard_map/ppermute | solution.py:473
  7.7 5.2 %copy-start.6 = (s32[2048,15]{0,1:T(8,128)S(1)}, s32[2048,15]{0,1:T(8,128)}, u32[]{:S(2)}) copy-start(s32[2048,15]{0,1:T(8,128)} %param.13) | copy-start | bytes 368644
  12.7 8.0 %collective-permute-start.3 = (bf16[512,256]{1,0:T(8,128)(2,1)S(1)}, bf16[512,256]{1,0:T(8,128)(2,1)S(1)}, u32[]{:S(2)}, u32[]{:S(2)}) collective-permute-start(bf16[512,256]{1,0:T(8,128)(2,1)S(1)} %get-tuple-element.23), channel_id=1, source_target_pairs={{0,1},{1,0},{2,3},{3,2},{4,5},{5,4},{6,7},{7,6},{8,9},{9,8},{10,11... | collective-permute-start | bytes 786440 | tf_op jit(solution)/shard_map/ppermute | solution.py:473
  12.8 9.2 %copy-start = (bf16[2048,768]{1,0:T(8,128)(2,1)S(1)}, bf16[2048,768]{1,0:T(8,128)(2,1)}, u32[]{:S(2)}) copy-start(bf16[2048,768]{1,0:T(8,128)(2,1)} %feats_ref.2) | copy-start | bytes 9437188
  20.2 9.3 %collective-permute-start = (bf16[1024,512]{1,0:T(8,128)(2,1)S(1)}, bf16[1024,512]{1,0:T(8,128)(2,1)S(1)}, u32[]{:S(2)}, u32[]{:S(2)}) collective-permute-start(bf16[1024,512]{1,0:T(8,128)(2,1)S(1)} %get-tuple-element.21), channel_id=1, source_target_pairs={{0,1},{1,0},{2,3},{3,2},{4,5},{5,4},{6,7},{7,6},{8,9},{9,8},{10,11... | collective-permute-start | bytes 3145736 | tf_op jit(solution)/shard_map/ppermute | solution.py:473
  20.9 8.3 %collective-permute-start.4 = (bf16[128,1024]{1,0:T(8,128)(2,1)S(1)}, bf16[128,1024]{1,0:T(8,128)(2,1)S(1)}, u32[]{:S(2)}, u32[]{:S(2)}) collective-permute-start(bf16[128,1024]{1,0:T(8,128)(2,1)S(1)} %pad_maximum_fusion.1), channel_id=1, source_target_pairs={{0,8},{8,0},{16,24},{24,16},{1,9},{9,1},{17,25},{25,17},{2,10},{10... | collective-permute-start | bytes 786440 | tf_op jit(solution)/shard_map/ppermute | solution.py:473
  21.5 8.0 %collective-permute-start.5 = (bf16[128,1024]{1,0:T(8,128)(2,1)S(1)}, bf16[128,1024]{1,0:T(8,128)(2,1)S(1)}, u32[]{:S(2)}, u32[]{:S(2)}) collective-permute-start(bf16[128,1024]{1,0:T(8,128)(2,1)S(1)} %pad_maximum_fusion.2), channel_id=1, source_target_pairs={{0,16},{8,24},{16,0},{24,8},{1,17},{9,25},{17,1},{25,9},{2,18},{10... | collective-permute-start | bytes 786440 | tf_op jit(solution)/shard_map/ppermute | solution.py:473
  31.2 1.8 %collective-permute-start.6 = (bf16[768,256]{1,0:T(8,128)(2,1)S(1)}, bf16[768,256]{1,0:T(8,128)(2,1)S(1)}, u32[]{:S(2)}, u32[]{:S(2)}) collective-permute-start(bf16[768,256]{1,0:T(8,128)(2,1)S(1)} %get-tuple-element.25), channel_id=1, source_target_pairs={{0,1},{1,0},{2,3},{3,2},{4,5},{5,4},{6,7},{7,6},{8,9},{9,8},{10,11... | collective-permute-start | bytes 1179656 | tf_op jit(solution)/shard_map/ppermute | solution.py:473
  31.2 6.0 %collective-permute-start.10 = (bf16[128,256]{1,0:T(8,128)(2,1)S(1)}, bf16[128,256]{1,0:T(8,128)(2,1)S(1)}, u32[]{:S(2)}, u32[]{:S(2)}) collective-permute-start(bf16[128,256]{1,0:T(8,128)(2,1)S(1)} %get-tuple-element.33), channel_id=1, source_target_pairs={{0,24},{8,16},{16,8},{24,0},{1,25},{9,17},{17,9},{25,1},{2,26},{10... | collective-permute-start | bytes 196616 | tf_op jit(solution)/shard_map/ppermute | solution.py:473
  33.6 6.3 %collective-permute-start.7 = (bf16[192,256]{1,0:T(8,128)(2,1)S(1)}, bf16[192,256]{1,0:T(8,128)(2,1)S(1)}, u32[]{:S(2)}, u32[]{:S(2)}) collective-permute-start(bf16[192,256]{1,0:T(8,128)(2,1)S(1)} %get-tuple-element.27), channel_id=1, source_target_pairs={{0,24},{1,25},{2,26},{3,27},{4,28},{5,29},{6,30},{7,31},{8,16},{9,... | collective-permute-start | bytes 294920 | tf_op jit(solution)/shard_map/ppermute | solution.py:495
  35.3 6.1 %collective-permute-start.8 = (bf16[192,256]{1,0:T(8,128)(2,1)S(1)}, bf16[192,256]{1,0:T(8,128)(2,1)S(1)}, u32[]{:S(2)}, u32[]{:S(2)}) collective-permute-start(bf16[192,256]{1,0:T(8,128)(2,1)S(1)} %get-tuple-element.28), channel_id=1, source_target_pairs={{0,8},{1,17},{2,10},{3,19},{4,12},{5,21},{6,14},{7,23},{8,0},{9,25... | collective-permute-start | bytes 294920 | tf_op jit(solution)/shard_map/ppermute | solution.py:495
  36.5 5.1 %collective-permute-start.9 = (bf16[192,256]{1,0:T(8,128)(2,1)S(1)}, bf16[192,256]{1,0:T(8,128)(2,1)S(1)}, u32[]{:S(2)}, u32[]{:S(2)}) collective-permute-start(bf16[192,256]{1,0:T(8,128)(2,1)S(1)} %get-tuple-element.29), channel_id=1, source_target_pairs={{0,16},{1,9},{2,18},{3,11},{4,20},{5,13},{6,22},{7,15},{8,24},{9,1... | collective-permute-start | bytes 294920 | tf_op jit(solution)/shard_map/ppermute | solution.py:495
  41.7 5.9 %collective-permute-start.11 = (bf16[320,256]{1,0:T(8,128)(2,1)S(1)}, bf16[320,256]{1,0:T(8,128)(2,1)S(1)}, u32[]{:S(2)}, u32[]{:S(2)}) collective-permute-start(bf16[320,256]{1,0:T(8,128)(2,1)S(1)} %pad_maximum_fusion.3), channel_id=1, source_target_pairs={{0,2},{1,5},{2,0},{3,7},{4,6},{5,1},{6,4},{7,3},{8,10},{9,13},{10,... | collective-permute-start | bytes 491528 | tf_op jit(solution)/shard_map/ppermute | solution.py:506
  47.6 6.4 %collective-permute-start.12 = (bf16[320,256]{1,0:T(8,128)(2,1)S(1)}, bf16[320,256]{1,0:T(8,128)(2,1)S(1)}, u32[]{:S(2)}, u32[]{:S(2)}) collective-permute-start(bf16[320,256]{1,0:T(8,128)(2,1)S(1)} %add_convert_fusion.2), channel_id=1, source_target_pairs={{0,4},{1,3},{2,6},{3,1},{4,0},{5,7},{6,2},{7,5},{8,12},{9,11},{10,... | collective-permute-start | bytes 491528 | tf_op jit(solution)/shard_map/ppermute | solution.py:506
  54.1 8.1 %collective-permute-start.15 = (bf16[320,256]{1,0:T(8,128)(2,1)S(1)}, bf16[320,256]{1,0:T(8,128)(2,1)S(1)}, u32[]{:S(2)}, u32[]{:S(2)}) collective-permute-start(bf16[320,256]{1,0:T(8,128)(2,1)S(1)} %add_convert_fusion.1), channel_id=1, source_target_pairs={{0,24},{1,25},{2,26},{3,27},{4,28},{5,29},{6,30},{7,31},{8,16},{9,... | collective-permute-start | bytes 491528 | tf_op jit(solution)/shard_map/ppermute | solution.py:495
  55.5 9.1 %collective-permute-start.16 = (bf16[320,256]{1,0:T(8,128)(2,1)S(1)}, bf16[320,256]{1,0:T(8,128)(2,1)S(1)}, u32[]{:S(2)}, u32[]{:S(2)}) collective-permute-start(bf16[320,256]{1,0:T(8,128)(2,1)S(1)} %add_convert_fusion.1), channel_id=1, source_target_pairs={{0,8},{1,17},{2,10},{3,19},{4,12},{5,21},{6,14},{7,23},{8,0},{9,25... | collective-permute-start | bytes 491528 | tf_op jit(solution)/shard_map/ppermute | solution.py:495
  58.2 6.6 %collective-permute-start.13 = (bf16[320,256]{1,0:T(8,128)(2,1)S(1)}, bf16[320,256]{1,0:T(8,128)(2,1)S(1)}, u32[]{:S(2)}, u32[]{:S(2)}) collective-permute-start(bf16[320,256]{1,0:T(8,128)(2,1)S(1)} %add_convert_fusion.1), channel_id=1, source_target_pairs={{0,16},{1,9},{2,18},{3,11},{4,20},{5,13},{6,22},{7,15},{8,24},{9,1... | collective-permute-start | bytes 491528 | tf_op jit(solution)/shard_map/ppermute | solution.py:495
  64.6 2.3 %collective-permute-start.17 = (bf16[640,256]{1,0:T(8,128)(2,1)S(1)}, bf16[640,256]{1,0:T(8,128)(2,1)S(1)}, u32[]{:S(2)}, u32[]{:S(2)}) collective-permute-start(bf16[640,256]{1,0:T(8,128)(2,1)S(1)} %constant_dynamic-update-slice_fusion.refs_1_), channel_id=1, source_target_pairs={{0,1},{1,0},{2,3},{3,2},{4,5},{5,4},{6,7},{7,6},{8,9},{9,8},{10,11... | collective-permute-start | bytes 983048 | tf_op jit(solution)/shard_map/ppermute | solution.py:473
  64.8 2.2 %collective-permute-start.14 = (bf16[640,256]{1,0:T(8,128)(2,1)S(1)}, bf16[640,256]{1,0:T(8,128)(2,1)S(1)}, u32[]{:S(2)}, u32[]{:S(2)}) collective-permute-start(bf16[640,256]{1,0:T(8,128)(2,1)S(1)} %pad_maximum_fusion.refs_0_), channel_id=1, source_target_pairs={{0,1},{1,0},{2,3},{3,2},{4,5},{5,4},{6,7},{7,6},{8,9},{9,8},{10,11... | collective-permute-start | bytes 983048 | tf_op jit(solution)/shard_map/ppermute | solution.py:473
where the time goes:
time: 68.8 us
  Pallas kernels  25.2 us (37%)
  starting transfers between devices  20.6 us (30%)
  waiting for transfers between devices  19.7 us (29%)
  between operations  1.69 us (2%)
  local copies, waits for them, and re-layouts  1.23 us (2%)
    ppermute x6, waiting for transfers between devices, trade(): lax.ppermute(arrays[turn], ('clique', 'copy'), route_of(n_clique, n_copy,...  10.8 us
    ppermute x10, starting transfers between devices, exchange(): lax.ppermute(array, axis, [(source, source ^ step) for source in range(si...  8.62 us
    ppermute x2, waiting for transfers between devices, sum_over_slice(): own = added(own, lax.ppermute(own, 'copy', route))  7.96 us
    ppermute x6, starting transfers between devices, trade(): lax.ppermute(arrays[turn], ('clique', 'copy'), route_of(n_clique, n_copy,...  7.64 us
    pallas_call x1, Pallas kernels, hot_sums(): pl.pallas_call(functools.partial(hot_kernel, 1.0 / fanout), in_specs=[who...  7.38 us
    pallas_call x1, Pallas kernels, cold_grad(): pl.pallas_call(functools.partial(cold_kernel, 1.0 / fanout), in_specs=[wh...  6.57 us
    pallas_call x1, Pallas kernels, row_gradients(): pl.pallas_call(functools.partial(rows_kernel, shard_rows.bit_length() - 1...  5.05 us
    ppermute x2, starting transfers between devices, sum_over_slice(): own = added(own, lax.ppermute(own, 'copy', route))  4.37 us
  transfers between devices with their start and end apart: 18, of which 10 were waited for; matrix products, arithmetic and copies ran while one was open for 0% of the time, Pallas kernels for 31%

commit v1 on v0

--- a/solution.py
+++ b/solution.py
@@ -76,11 +76,13 @@
     shift = q_rows.bit_length() - 1
     low = index & (q_rows - 1)
     one = jnp.left_shift(jnp.ones_like(index), (index >> shift) * 4)
+    spare = -terms % 8
+    low = jnp.concatenate([low, jnp.full((spare, 128), -1, jnp.int32)], axis=0)
+    one = jnp.concatenate([one, jnp.zeros((spare, 128), jnp.int32)], axis=0)
     unit = one
-    for other in range(1, terms):
-        turned_low = jnp.concatenate([low[other:], low[:other]], axis=0)
-        turned = jnp.concatenate([one[other:], one[:other]], axis=0)
-        unit = unit + jnp.where(turned_low == low, turned, jnp.zeros_like(turned))
+    for other in range(1, terms + spare):
+        same = pltpu.roll(low, other, 0) == low
+        unit = unit + jnp.where(same, pltpu.roll(one, other, 0), jnp.zeros_like(one))
     tall = min(256, q_rows) // TILE
     shape = (tall, TILE, 128)
     place = lax.broadcasted_iota(jnp.int32, shape, 0) * TILE + lax.broadcasted_iota(jnp.int32, shape, 1)
@@ -98,15 +100,13 @@
         store(top, tall, word)
 
 
-def unpack(word_ref, field, count_ref, part=0, parts=1):
-    deep = word_ref.shape[0] // parts
-    words = word_ref[part * deep : (part + 1) * deep, :, :]
+def unpack(word_ref, field, lanes, count_ref):
+    words = word_ref[:, :, lanes]
     if field < FIELDS - 1:
         counts = words & (15 << (4 * field))
     else:
         counts = (words >> (4 * field)) & 15
-    rows = deep * TILE
-    count_ref[part * rows : (part + 1) * rows, :] = counts.astype(BF16).reshape(rows, count_ref.shape[1])
+    count_ref[...] = counts.astype(BF16).reshape(count_ref.shape)
 
 
 def unpacked_scale(field):
@@ -115,13 +115,10 @@
 
 def rows_kernel(
     shard_bits, half_rows, chunks, members,
-    place_ref, count_ref, index_in, out_grad_ref, pre_act_in, layer_two_in,
-    row_grad_out, own_ref, send_ref, word_out,
-    index_ref, masked_ref, pre_act_ref, layer_two_ref, row_grad_ref, word_ref, sum_ref,
+    place_ref, count_ref, index_ref, out_grad_ref, pre_act_ref, layer_two_ref,
+    row_grad_ref, own_ref, send_ref, word_ref,
+    masked_ref, sum_ref,
 ):
-    index_ref[...] = index_in[...]
-    pre_act_ref[...] = pre_act_in[...]
-    layer_two_ref[...] = layer_two_in[...]
     rows = out_grad_ref.shape[0] // chunks
     blocks = [slice(chunk * rows, (chunk + 1) * rows) for chunk in range(chunks)]
     own_shard, own_core = place_ref[0], place_ref[1]
@@ -169,8 +166,6 @@
         sum_ref[...] = part if chunk == 0 else sum_ref[...] + part
         for tile in range(ends[chunk], ends[chunk + 1]):
             build(tile)
-    row_grad_out[...] = row_grad_ref[...]
-    word_out[...] = word_ref[...]
     halves(sum_ref, own_ref, send_ref, own_shard, own_core, members)
 
 
@@ -197,12 +192,7 @@
             jax.ShapeDtypeStruct((deep, TILE, rows), I16),
         ],
         scratch_shapes=[
-            pltpu.VMEM(index.shape, jnp.int32),
             pltpu.VMEM((rows, d_out), BF16),
-            pltpu.VMEM((rows, d_h), BF16),
-            pltpu.VMEM((d_h, d_out), BF16),
-            pltpu.VMEM((rows, d_h), BF16),
-            pltpu.VMEM((deep, TILE, rows), I16),
             pltpu.VMEM((d_h, d_out), F32),
         ],
         compiler_params=params(ROWS_MIB),
@@ -211,17 +201,15 @@
     )(place, batch_count, index, out_grad, pre_act, layer_two)
 
 
-def sums_of_field(counts, row_grad_ref, field, scale, out_ref, top, beside):
-    tall = counts[0].shape[0]
-    wide = row_grad_ref.shape[1] // 2
-    for half in range(2):
-        lanes = slice(half * wide, (half + 1) * wide)
-        found = jnp.dot(
-            counts[field % 2][...], row_grad_ref[:, lanes], preferred_element_type=F32
-        )
-        found = found * (scale / unpacked_scale(field))
-        out_ref[top : top + tall, lanes] = found.astype(BF16)
-        beside(half)
+def build_tiles(index_ref, word_ref, first, count, word_first):
+    for tile in range(count):
+        here = slice((first + tile) * 128, (first + tile + 1) * 128)
+        lanes = slice((word_first + tile) * 128, (word_first + tile + 1) * 128)
+
+        def store(top, deep, words, lanes=lanes):
+            word_ref[top : top + deep, :, lanes] = words
+
+        build_words(index_ref[:, here], word_ref.shape[0] * TILE, store)
 
 
 def hot_kernel(
@@ -232,23 +220,15 @@
     row_grad_ref[...] = row_grad_in[...]
     index_ref[...] = index_in[...]
     tall, rows = counts[0].shape
-    tiles = rows // 128 // FIELDS // 2
-    unpack(word_ref, 0, counts[0])
+    tiles = rows // 128 // 2 // FIELDS
+    unpack(word_ref, 0, slice(None), counts[0])
     for field in range(FIELDS):
-
-        def beside(half, field=field):
-            if field + 1 < FIELDS:
-                unpack(word_ref, field + 1, counts[(field + 1) % 2], half, 2)
-            first = (2 * field + half) * tiles
-            for tile in range(first, first + tiles):
-                lanes = slice(tile * 128, (tile + 1) * 128)
-
-                def store(top, deep, words, lanes=lanes):
-                    cold_word_ref[top : top + deep, :, lanes] = words
-
-                build_words(index_ref[:, lanes], cold_word_ref.shape[0] * TILE, store)
-
-        sums_of_field(counts, row_grad_ref, field, scale, sums_ref, field * tall, beside)
+        found = jnp.dot(counts[field % 2][...], row_grad_ref[...], preferred_element_type=F32)
+        found = found * (scale / unpacked_scale(field))
+        sums_ref[field * tall : (field + 1) * tall, :] = found.astype(BF16)
+        if field + 1 < FIELDS:
+            unpack(word_ref, field + 1, slice(None), counts[(field + 1) % 2])
+        build_tiles(index_ref, cold_word_ref, field * tiles, tiles, field * tiles)
     send_ref[...] = sums_ref[: 2 * tall, :]
     keep_ref[...] = sums_ref[2 * tall :, :]
     cold_word_out[...] = cold_word_ref[...]
@@ -265,14 +245,14 @@
         out_shape=[
             half,
             half,
-            jax.ShapeDtypeStruct((cold_rows // FIELDS // TILE, TILE, rows), I16),
+            jax.ShapeDtypeStruct((cold_rows // FIELDS // TILE, TILE, rows // 2), I16),
         ],
         scratch_shapes=[
             pltpu.VMEM(words.shape, I16),
             pltpu.VMEM(row_grad.shape, BF16),
             pltpu.VMEM(cold_index.shape, jnp.int32),
             pltpu.VMEM((q_rows * FIELDS, d_h), BF16),
-            pltpu.VMEM((cold_rows // FIELDS // TILE, TILE, rows), I16),
+            pltpu.VMEM((cold_rows // FIELDS // TILE, TILE, rows // 2), I16),
             pltpu.VMEM((q_rows, rows), BF16),
             pltpu.VMEM((q_rows, rows), BF16),
         ],
@@ -283,61 +263,71 @@
 
 
 def cold_kernel(
-    scale, word_in, row_grad_in, feats_ref, grad_out,
-    word_ref, row_grad_ref, grad_ref, sums_ref, held_ref, sem, *counts
+    scale, word_in, index_in, row_grad_in, feats_ref, grad_out,
+    word_ref, index_ref, row_grad_ref, grad_ref, part_ref, sums_ref, held_ref, sem, *counts
 ):
     fetch = pltpu.make_async_copy(feats_ref, held_ref, sem)
     fetch.start()
-    word_ref[...] = word_in[...]
+    tall, half = counts[0].shape
+    word_ref[:, :, :half] = word_in[...]
+    index_ref[...] = index_in[...]
     row_grad_ref[...] = row_grad_in[...]
-    tall = counts[0].shape[0]
-    wide = held_ref.shape[1] // 2
-
-    def add_product(field, half):
-        rows, lanes = slice(field * tall, (field + 1) * tall), slice(half * wide, (half + 1) * wide)
-        part = transposed_dot(held_ref[rows, lanes], sums_ref[rows, :])
-        grad_ref[lanes, :] = part if field == 0 else grad_ref[lanes, :] + part
-
-    unpack(word_ref, 0, counts[0])
-    for field in range(FIELDS):
-        if field == 1:
+    tiles = half // 128 // FIELDS
+
+    def add_product(field):
+        rows = slice(field * tall, (field + 1) * tall)
+        part = transposed_dot(held_ref[rows, :], sums_ref[rows, :])
+        grad_ref[...] = part if field == 0 else grad_ref[...] + part
+
+    steps = [(k, field) for k in range(2) for field in range(FIELDS)]
+    unpack(word_ref, 0, slice(half), counts[0])
+    for step, (k, field) in enumerate(steps):
+        depth, rows = slice(k * half, (k + 1) * half), slice(field * tall, (field + 1) * tall)
+        found = jnp.dot(counts[step % 2][...], row_grad_ref[depth, :], preferred_element_type=F32)
+        if k == 0:
+            part_ref[rows, :] = found
+            first = half // 128 + field * tiles
+            build_tiles(index_ref, word_ref, first, tiles, first)
+        else:
+            found = (part_ref[rows, :] + found) * (scale / unpacked_scale(field))
+            sums_ref[rows, :] = found.astype(BF16)
+        if step + 1 < len(steps):
+            ahead, next_field = steps[step + 1]
+            lanes = slice(ahead * half, (ahead + 1) * half)
+            unpack(word_ref, next_field, lanes, counts[(step + 1) % 2])
+        if k == 1 and field == 0:
             fetch.wait()
-
-        def beside(half, field=field):
-            if field + 1 < FIELDS:
-                unpack(word_ref, field + 1, counts[(field + 1) % 2], half, 2)
-            if field > 0:
-                add_product(field - 1, half)
-
-        sums_of_field(counts, row_grad_ref, field, scale, sums_ref, field * tall, beside)
-    for half in range(2):
-        add_product(FIELDS - 1, half)
+        if k == 1 and field > 0:
+            add_product(field - 1)
+    add_product(FIELDS - 1)
     grad_out[...] = grad_ref[...]
 
 
-def cold_grad(words, row_grad, feats, fanout):
+def cold_grad(words, index, row_grad, feats, fanout):
     rows, d_h = row_grad.shape
     cold_rows, d_in = feats.shape
     q_rows = cold_rows // FIELDS
     return pl.pallas_call(
         functools.partial(cold_kernel, 1.0 / fanout),
-        in_specs=[whole(), whole(), in_place()],
+        in_specs=[whole(), whole(), whole(), in_place()],
         out_specs=whole(),
         out_shape=jax.ShapeDtypeStruct((d_in, d_h), F32),
         scratch_shapes=[
-            pltpu.VMEM(words.shape, I16),
+            pltpu.VMEM((q_rows // TILE, TILE, rows), I16),
+            pltpu.VMEM(index.shape, jnp.int32),
             pltpu.VMEM(row_grad.shape, BF16),
             pltpu.VMEM((d_in, d_h), F32),
+            pltpu.VMEM((cold_rows, d_h), F32),
             pltpu.VMEM((cold_rows, d_h), BF16),
             pltpu.VMEM((cold_rows, d_in), BF16),
             pltpu.SemaphoreType.DMA,
-            pltpu.VMEM((q_rows, rows), BF16),
-            pltpu.VMEM((q_rows, rows), BF16),
+            pltpu.VMEM((q_rows, rows // 2), BF16),
+            pltpu.VMEM((q_rows, rows // 2), BF16),
         ],
         compiler_params=params(40),
         cost_estimate=cost(10**10, 10**8),
         name="cold_grad",
-    )(words, row_grad, feats)
+    )(words, index, row_grad, feats)
 
 
 def join_kernel(parts, place_ref, cold_ref, keep_ref, other_ref, *rest):
@@ -543,7 +533,7 @@
     feats, two = gather(half_feats, two)
     send, keep, words = hot_sums(words, row_grad, cold_index.T, cold_rows, fanout)
     other = exchange(send, "copy", 1)
-    cold = cold_grad(words, row_grad, cold_feats, fanout)
+    cold = cold_grad(words, cold_index.T, row_grad, cold_feats, fanout)
     own_one, twin_one = join(place, cold, keep, other, feats)
     shares = pair_sums(place, own_one, exchange(twin_one, "copy", 1), n_clique)
     shares = sum_over_slice(shares, two)

time: 68.8 us -> 68.2 us (level)
    ppermute x2, waiting for transfers between devices: 7.96 us -> 9.54 us  [sum_over_slice(): own = added(own, lax.ppermute(own, 'copy', route))]
    pallas_call x1, Pallas kernels: 7.38 us -> 5.92 us  [hot_sums(): pl.pallas_call(functools.partial(hot_kernel, 1.0 / fanout), in_specs=[who...]
    pallas_call x1, Pallas kernels: 6.57 us -> 7.97 us  [cold_grad(): pl.pallas_call(functools.partial(cold_kernel, 1.0 / fanout), in_specs=[wh...]
    ppermute x6, waiting for transfers between devices: 10.8 us -> 9.77 us  [trade(): lax.ppermute(arrays[turn], ('clique', 'copy'), route_of(n_clique, n_copy,...]
    ppermute x10, starting transfers between devices: 8.62 us -> 9.52 us  [exchange(): lax.ppermute(array, axis, [(source, source ^ step) for source in range(si...]
    ppermute x10, waiting for transfers between devices: 0.91 us -> 0.03 us  [exchange(): lax.ppermute(array, axis, [(source, source ^ step) for source in range(si...]
    ppermute x2, starting transfers between devices: 4.37 us -> 3.66 us  [sum_over_slice(): own = added(own, lax.ppermute(own, 'copy', route))]
  transfers between devices with their start and end apart: 18 -> 18, of which waited for: 10 -> 7; matrix products, arithmetic and copies ran while one was open for 0% -> 0% of each run, Pallas kernels for 31% -> 31%
where the time goes in v1:
time: 68.2 us; the launch traced here: 67.9 us
  Pallas kernels  25 us (37%)
  starting transfers between devices  20.3 us (30%)
  waiting for transfers between devices  19.3 us (28%)
  between operations  1.73 us (3%)
  local copies, waits for them, and re-layouts  1.23 us (2%)
    ppermute x6, waiting for transfers between devices, trade(): lax.ppermute(arrays[turn], ('clique', 'copy'), route_of(n_clique, n_copy,...  9.77 us
    ppermute x2, waiting for transfers between devices, sum_over_slice(): own = added(own, lax.ppermute(own, 'copy', route))  9.54 us
    ppermute x10, starting transfers between devices, exchange(): lax.ppermute(array, axis, [(source, source ^ step) for source in range(si...  9.52 us
    pallas_call x1, Pallas kernels, cold_grad(): pl.pallas_call(functools.partial(cold_kernel, 1.0 / fanout), in_specs=[wh...  7.97 us
    ppermute x6, starting transfers between devices, trade(): lax.ppermute(arrays[turn], ('clique', 'copy'), route_of(n_clique, n_copy,...  7.11 us
    pallas_call x1, Pallas kernels, hot_sums(): pl.pallas_call(functools.partial(hot_kernel, 1.0 / fanout), in_specs=[who...  5.92 us
    pallas_call x1, Pallas kernels, row_gradients(): pl.pallas_call(functools.partial(rows_kernel, shard_rows.bit_length() - 1...  4.88 us
    ppermute x2, starting transfers between devices, sum_over_slice(): own = added(own, lax.ppermute(own, 'copy', route))  3.66 us
  transfers between devices with their start and end apart: 18, of which 7 were waited for; matrix products, arithmetic and copies ran while one was open for 0% of the time, Pallas kernels for 31%

profile of v1, /device:TPU:0, one launch (start us, length us, event | category | flops | bytes accessed | tf_op | source)
XLA Modules:
  0.0 67.9 jit_solution(3228402998673850671)
XLA Ops:
  0.6 0.1 pad_add_fusion.place_ref
  0.7 1.1 %copy-done.3 = bf16[512,768]{1,0:T(8,128)(2,1)S(1)} copy-done((bf16[512,768]{1,0:T(8,128)(2,1)S(1)}, bf16[512,768]{1,0:T(8,128)(2,1)}, u32[]{:S(2)}) %copy-start.3) | copy-done | bytes 786456
  1.9 0.6 half_of.1.rest_0_
  2.4 3.0 %collective-permute-start.2 = (bf16[256,768]{1,0:T(8,128)(2,1)S(1)}, bf16[256,768]{1,0:T(8,128)(2,1)S(1)}, u32[]{:S(2)}, u32[]{:S(2)}) collective-permute-start(bf16[256,768]{1,0:T(8,128)(2,1)S(1)} %half_of.1.rest_0_), channel_id=1, source_target_pairs={{0,16},{8,24},{16,0},{24,8},{1,17},{9,25},{17,1},{25,9},{2,18},{10... | collective-permute-start | bytes 1179656 | tf_op jit(solution)/shard_map/ppermute | solution.py:463
  5.5 1.5 %collective-permute-start.1 = (bf16[256,768]{1,0:T(8,128)(2,1)S(1)}, bf16[256,768]{1,0:T(8,128)(2,1)S(1)}, u32[]{:S(2)}, u32[]{:S(2)}) collective-permute-start(bf16[256,768]{1,0:T(8,128)(2,1)S(1)} %half_of.1.rest_0_), channel_id=1, source_target_pairs={{0,8},{8,0},{16,24},{24,16},{1,9},{9,1},{17,25},{25,17},{2,10},{10... | collective-permute-start | bytes 1179656 | tf_op jit(solution)/shard_map/ppermute | solution.py:463
  7.7 0.0 copy-start.6
  7.7 4.9 %row_gradients.1 = (bf16[2048,512]{1,0:T(8,128)(2,1)S(1)}, bf16[512,256]{1,0:T(8,128)(2,1)S(1)}, bf16[512,256]{1,0:T(8,128)(2,1)S(1)}, s16[32,16,2048]{2,1,0:T(8,128)(2,1)S(1)}) custom-call(s32[2]{0:T(128)S(1)} %pad_add_fusion.place_ref, s32[1]{0:T(128)S(6)} %copy.15.count_ref, s32[10,2048]{1,0:T(8,128)S(1)} %bitcast.4, bf16[2048,512]{1,0:T(8,128)(2,1)S(1)} %copy-done.1, ...), custom_call_target="tpu_custom_call" | custom-call | flops 10000000000 | bytes 100000000 | tf_op jit(solution)/shard_map/row_gradients/pallas_call | solution.py:178
  12.6 0.1 collective-permute-start.3
  12.6 0.0 copy-start
  12.7 5.9 %hot_sums.1 = (bf16[1024,512]{1,0:T(8,128)(2,1)S(1)}, bf16[1024,512]{1,0:T(8,128)(2,1)S(1)}, s16[32,16,1024]{2,1,0:T(8,128)(2,1)S(1)}) custom-call(s16[32,16,2048]{2,1,0:T(8,128)(2,1)S(1)} %get-tuple-element.17.word_in, bf16[2048,512]{1,0:T(8,128)(2,1)S(1)} %get-tuple-element.18.row_grad_in, s32[15,2048]{1,0:T(8,128)S(1)} %bitcast.5), custom_call_target="tpu_custom_call" | custom-call | flops 10000000000 | bytes 100000000 | tf_op jit(solution)/shard_map/hot_sums/pallas_call | solution.py:241
  18.6 0.5 collective-permute-start
  19.1 0.0 collective-permute-done.3
  19.1 0.1 add_convert_fusion
  19.2 0.0 collective-permute-done.2.rest_2_
  19.3 0.5 collective-permute-start.4
  19.8 0.0 collective-permute-done.1.rest_1_
  19.9 0.5 collective-permute-start.5
  20.3 8.0 %cold_grad.1.cold_ref = f32[768,512]{1,0:T(8,128)S(1)} custom-call(s16[32,16,1024]{2,1,0:T(8,128)(2,1)S(1)} %get-tuple-element.19.word_in, s32[15,2048]{1,0:T(8,128)S(1)} %bitcast.6, bf16[2048,512]{1,0:T(8,128)(2,1)S(1)} %get-tuple-element.18.row_grad_in, bf16[2048,768]{1,0:T(8,128)(2,1)S(1)} %copy-done), custom_call_target="tpu_custom_call" | custom-call | flops 10000000000 | bytes 100000000 | tf_op jit(solution)/shard_map/cold_grad/pallas_call | solution.py:310
  28.3 0.0 collective-permute-done.4.rest_3_
  28.3 0.0 collective-permute-done.5.rest_4_
  28.3 0.0 collective-permute-done.other_ref
  28.4 1.6 %join.1 = (bf16[768,256]{1,0:T(8,128)(2,1)S(1)}, bf16[768,256]{1,0:T(8,128)(2,1)S(1)}) custom-call(s32[2]{0:T(128)S(1)} %pad_add_fusion.place_ref, f32[768,512]{1,0:T(8,128)S(1)} %cold_grad.1.cold_ref, bf16[1024,512]{1,0:T(8,128)(2,1)S(1)} %get-tuple-element.20.keep_ref, bf16[1024,512]{1,0:T(8,128)(2,1)S(1)} %collective-permute-done.other_ref, ...), custom_call_target="tpu_custom_call" | custom-call | flops 805306368 | bytes 1572864 | tf_op jit(solution)/shard_map/join/pallas_call | solution.py:368
  30.0 0.1 collective-permute-start.6
  30.1 2.7 %collective-permute-start.10 = (bf16[128,256]{1,0:T(8,128)(2,1)S(1)}, bf16[128,256]{1,0:T(8,128)(2,1)S(1)}, u32[]{:S(2)}, u32[]{:S(2)}) collective-permute-start(bf16[128,256]{1,0:T(8,128)(2,1)S(1)} %get-tuple-element.33), channel_id=1, source_target_pairs={{0,24},{8,16},{16,8},{24,0},{1,25},{9,17},{17,9},{25,1},{2,26},{10... | collective-permute-start | bytes 196616 | tf_op jit(solution)/shard_map/ppermute | solution.py:463
  32.8 0.0 collective-permute-done.6.other_ref
  32.8 0.6 pair_sums.1
  33.4 1.7 %collective-permute-start.7 = (bf16[192,256]{1,0:T(8,128)(2,1)S(1)}, bf16[192,256]{1,0:T(8,128)(2,1)S(1)}, u32[]{:S(2)}, u32[]{:S(2)}) collective-permute-start(bf16[192,256]{1,0:T(8,128)(2,1)S(1)} %get-tuple-element.27), channel_id=1, source_target_pairs={{0,24},{1,25},{2,26},{3,27},{4,28},{5,29},{6,30},{7,31},{8,16},{9,... | collective-permute-start | bytes 294920 | tf_op jit(solution)/shard_map/ppermute | solution.py:485
  35.1 0.5 collective-permute-start.8
  35.6 1.4 %collective-permute-start.9 = (bf16[192,256]{1,0:T(8,128)(2,1)S(1)}, bf16[192,256]{1,0:T(8,128)(2,1)S(1)}, u32[]{:S(2)}, u32[]{:S(2)}) collective-permute-start(bf16[192,256]{1,0:T(8,128)(2,1)S(1)} %get-tuple-element.29), channel_id=1, source_target_pairs={{0,16},{1,9},{2,18},{3,11},{4,20},{5,13},{6,22},{7,15},{8,24},{9,1... | collective-permute-start | bytes 294920 | tf_op jit(solution)/shard_map/ppermute | solution.py:485
  37.0 2.7 %collective-permute-done.7 = bf16[192,256]{1,0:T(8,128)(2,1)S(1)} collective-permute-done((bf16[192,256]{1,0:T(8,128)(2,1)S(1)}, bf16[192,256]{1,0:T(8,128)(2,1)S(1)}, u32[]{:S(2)}, u32[]{:S(2)}) %collective-permute-start.7) | collective-permute-done | bytes 98336 | tf_op jit(solution)/shard_map/ppermute | solution.py:485
  39.8 0.7 %collective-permute-done.8 = bf16[192,256]{1,0:T(8,128)(2,1)S(1)} collective-permute-done((bf16[192,256]{1,0:T(8,128)(2,1)S(1)}, bf16[192,256]{1,0:T(8,128)(2,1)S(1)}, u32[]{:S(2)}, u32[]{:S(2)}) %collective-permute-start.8) | collective-permute-done | bytes 98336 | tf_op jit(solution)/shard_map/ppermute | solution.py:485
  40.5 0.9 %collective-permute-done.9 = bf16[192,256]{1,0:T(8,128)(2,1)S(1)} collective-permute-done((bf16[192,256]{1,0:T(8,128)(2,1)S(1)}, bf16[192,256]{1,0:T(8,128)(2,1)S(1)}, u32[]{:S(2)}, u32[]{:S(2)}) %collective-permute-start.9) | collective-permute-done | bytes 98336 | tf_op jit(solution)/shard_map/ppermute | solution.py:485
  41.3 0.1 add_convert_fusion.3
  41.4 1.6 %collective-permute-start.11 = (bf16[320,256]{1,0:T(8,128)(2,1)S(1)}, bf16[320,256]{1,0:T(8,128)(2,1)S(1)}, u32[]{:S(2)}, u32[]{:S(2)}) collective-permute-start(bf16[320,256]{1,0:T(8,128)(2,1)S(1)} %pad_maximum_fusion.3), channel_id=1, source_target_pairs={{0,2},{1,5},{2,0},{3,7},{4,6},{5,1},{6,4},{7,3},{8,10},{9,13},{10,... | collective-permute-start | bytes 491528 | tf_op jit(solution)/shard_map/ppermute | solution.py:496
  43.0 5.0 %collective-permute-done.11 = bf16[320,256]{1,0:T(8,128)(2,1)S(1)} collective-permute-done((bf16[320,256]{1,0:T(8,128)(2,1)S(1)}, bf16[320,256]{1,0:T(8,128)(2,1)S(1)}, u32[]{:S(2)}, u32[]{:S(2)}) %collective-permute-start.11) | collective-permute-done | bytes 163872 | tf_op jit(solution)/shard_map/ppermute | solution.py:496
  48.1 2.1 %collective-permute-start.12 = (bf16[320,256]{1,0:T(8,128)(2,1)S(1)}, bf16[320,256]{1,0:T(8,128)(2,1)S(1)}, u32[]{:S(2)}, u32[]{:S(2)}) collective-permute-start(bf16[320,256]{1,0:T(8,128)(2,1)S(1)} %add_convert_fusion.2), channel_id=1, source_target_pairs={{0,4},{1,3},{2,6},{3,1},{4,0},{5,7},{6,2},{7,5},{8,12},{9,11},{10,... | collective-permute-start | bytes 491528 | tf_op jit(solution)/shard_map/ppermute | solution.py:496
  50.1 4.5 %collective-permute-done.12 = bf16[320,256]{1,0:T(8,128)(2,1)S(1)} collective-permute-done((bf16[320,256]{1,0:T(8,128)(2,1)S(1)}, bf16[320,256]{1,0:T(8,128)(2,1)S(1)}, u32[]{:S(2)}, u32[]{:S(2)}) %collective-permute-start.12) | collective-permute-done | bytes 163872 | tf_op jit(solution)/shard_map/ppermute | solution.py:496
  54.7 1.6 %collective-permute-start.15 = (bf16[320,256]{1,0:T(8,128)(2,1)S(1)}, bf16[320,256]{1,0:T(8,128)(2,1)S(1)}, u32[]{:S(2)}, u32[]{:S(2)}) collective-permute-start(bf16[320,256]{1,0:T(8,128)(2,1)S(1)} %add_convert_fusion.1), channel_id=1, source_target_pairs={{0,24},{1,25},{2,26},{3,27},{4,28},{5,29},{6,30},{7,31},{8,16},{9,... | collective-permute-start | bytes 491528 | tf_op jit(solution)/shard_map/ppermute | solution.py:485
  56.3 0.0 collective-permute-start.16
  56.3 2.0 %collective-permute-start.13 = (bf16[320,256]{1,0:T(8,128)(2,1)S(1)}, bf16[320,256]{1,0:T(8,128)(2,1)S(1)}, u32[]{:S(2)}, u32[]{:S(2)}) collective-permute-start(bf16[320,256]{1,0:T(8,128)(2,1)S(1)} %add_convert_fusion.1), channel_id=1, source_target_pairs={{0,16},{1,9},{2,18},{3,11},{4,20},{5,13},{6,22},{7,15},{8,24},{9,1... | collective-permute-start | bytes 491528 | tf_op jit(solution)/shard_map/ppermute | solution.py:485
  58.3 3.5 %collective-permute-done.15 = bf16[320,256]{1,0:T(8,128)(2,1)S(1)} collective-permute-done((bf16[320,256]{1,0:T(8,128)(2,1)S(1)}, bf16[320,256]{1,0:T(8,128)(2,1)S(1)}, u32[]{:S(2)}, u32[]{:S(2)}) %collective-permute-start.15) | collective-permute-done | bytes 163872 | tf_op jit(solution)/shard_map/ppermute | solution.py:485
  61.8 1.9 %collective-permute-done.16 = bf16[320,256]{1,0:T(8,128)(2,1)S(1)} collective-permute-done((bf16[320,256]{1,0:T(8,128)(2,1)S(1)}, bf16[320,256]{1,0:T(8,128)(2,1)S(1)}, u32[]{:S(2)}, u32[]{:S(2)}) %collective-permute-start.16) | collective-permute-done | bytes 163872 | tf_op jit(solution)/shard_map/ppermute | solution.py:485
  63.7 0.1 collective-permute-start.17
  63.8 0.0 collective-permute-done.13
  63.8 0.5 collective-permute-start.14
  64.4 1.7 %lay.2 = (f32[768,512]{1,0:T(8,128)}, f32[512,512]{1,0:T(8,128)}) custom-call(s32[2]{0:T(128)S(1)} %pad_add_fusion.place_ref, bf16[640,256]{1,0:T(8,128)(2,1)S(1)} %pad_maximum_fusion.refs_0_, bf16[640,256]{1,0:T(8,128)(2,1)S(1)} %constant_dynamic-update-slice_fusion.refs_1_), custom_call_target="tpu_custom_call" | custom-call | flops 10000000000 | bytes 100000000 | tf_op jit(solution)/shard_map/lay/pallas_call | solution.py:447
  66.1 0.0 collective-permute-done.14.refs_0_
  66.1 1.7 %lay.3 = (f32[768,512]{1,0:T(8,128)}, f32[512,512]{1,0:T(8,128)}) custom-call(s32[2]{0:T(128)S(1)} %pad_add_fusion.place_ref, bf16[640,256]{1,0:T(8,128)(2,1)S(1)} %collective-permute-done.14.refs_0_, bf16[640,256]{1,0:T(8,128)(2,1)S(1)} %collective-permute-done.17.refs_1_, ...), custom_call_target="tpu_custom_call", output_to_operand_aliasing={{0}: (3, {}), {1}: (4, {})} | custom-call | flops 10000000000 | bytes 100000000 | tf_op jit(solution)/shard_map/lay/pallas_call | solution.py:447
  (25 shorter events, 0.3 us)
Async XLA Ops:
  0.7 1.1 %copy-start.3 = (bf16[512,768]{1,0:T(8,128)(2,1)S(1)}, bf16[512,768]{1,0:T(8,128)(2,1)}, u32[]{:S(2)}) copy-start(bf16[512,768]{1,0:T(8,128)(2,1)} %feats_ref.3) | copy-start | bytes 2359300
  1.8 5.8 %copy-start.1 = (bf16[2048,512]{1,0:T(8,128)(2,1)S(1)}, bf16[2048,512]{1,0:T(8,128)(2,1)}, u32[]{:S(2)}) copy-start(bf16[2048,512]{1,0:T(8,128)(2,1)} %out_grad_ref.1) | copy-start | bytes 6291460
  1.8 5.8 %copy-start.2 = (bf16[2048,512]{1,0:T(8,128)(2,1)S(1)}, bf16[2048,512]{1,0:T(8,128)(2,1)}, u32[]{:S(2)}) copy-start(bf16[2048,512]{1,0:T(8,128)(2,1)} %pre_act_ref.1) | copy-start | bytes 6291460
  1.8 5.8 %copy-start.4 = (bf16[512,512]{1,0:T(8,128)(2,1)S(1)}, bf16[512,512]{1,0:T(8,128)(2,1)}, u32[]{:S(2)}) copy-start(bf16[512,512]{1,0:T(8,128)(2,1)} %layer_two_ref.1) | copy-start | bytes 1572868
  1.9 5.8 %copy-start.5 = (s32[2048,10]{0,1:T(8,128)S(1)}, s32[2048,10]{0,1:T(8,128)}, u32[]{:S(2)}) copy-start(s32[2048,10]{0,1:T(8,128)} %param.12) | copy-start | bytes 245764
  2.4 16.8 %collective-permute-start.2 = (bf16[256,768]{1,0:T(8,128)(2,1)S(1)}, bf16[256,768]{1,0:T(8,128)(2,1)S(1)}, u32[]{:S(2)}, u32[]{:S(2)}) collective-permute-start(bf16[256,768]{1,0:T(8,128)(2,1)S(1)} %half_of.1.rest_0_), channel_id=1, source_target_pairs={{0,16},{8,24},{16,0},{24,8},{1,17},{9,25},{17,1},{25,9},{2,18},{10... | collective-permute-start | bytes 1179656 | tf_op jit(solution)/shard_map/ppermute | solution.py:463
  5.5 14.3 %collective-permute-start.1 = (bf16[256,768]{1,0:T(8,128)(2,1)S(1)}, bf16[256,768]{1,0:T(8,128)(2,1)S(1)}, u32[]{:S(2)}, u32[]{:S(2)}) collective-permute-start(bf16[256,768]{1,0:T(8,128)(2,1)S(1)} %half_of.1.rest_0_), channel_id=1, source_target_pairs={{0,8},{8,0},{16,24},{24,16},{1,9},{9,1},{17,25},{25,17},{2,10},{10... | collective-permute-start | bytes 1179656 | tf_op jit(solution)/shard_map/ppermute | solution.py:463
  7.7 5.0 %copy-start.6 = (s32[2048,15]{0,1:T(8,128)S(1)}, s32[2048,15]{0,1:T(8,128)}, u32[]{:S(2)}) copy-start(s32[2048,15]{0,1:T(8,128)} %param.13) | copy-start | bytes 368644
  12.6 6.6 %collective-permute-start.3 = (bf16[512,256]{1,0:T(8,128)(2,1)S(1)}, bf16[512,256]{1,0:T(8,128)(2,1)S(1)}, u32[]{:S(2)}, u32[]{:S(2)}) collective-permute-start(bf16[512,256]{1,0:T(8,128)(2,1)S(1)} %get-tuple-element.23), channel_id=1, source_target_pairs={{0,1},{1,0},{2,3},{3,2},{4,5},{5,4},{6,7},{7,6},{8,9},{9,8},{10,11... | collective-permute-start | bytes 786440 | tf_op jit(solution)/shard_map/ppermute | solution.py:463
  12.6 7.7 %copy-start = (bf16[2048,768]{1,0:T(8,128)(2,1)S(1)}, bf16[2048,768]{1,0:T(8,128)(2,1)}, u32[]{:S(2)}) copy-start(bf16[2048,768]{1,0:T(8,128)(2,1)} %feats_ref.2) | copy-start | bytes 9437188
  18.6 9.8 %collective-permute-start = (bf16[1024,512]{1,0:T(8,128)(2,1)S(1)}, bf16[1024,512]{1,0:T(8,128)(2,1)S(1)}, u32[]{:S(2)}, u32[]{:S(2)}) collective-permute-start(bf16[1024,512]{1,0:T(8,128)(2,1)S(1)} %get-tuple-element.21), channel_id=1, source_target_pairs={{0,1},{1,0},{2,3},{3,2},{4,5},{5,4},{6,7},{7,6},{8,9},{9,8},{10,11... | collective-permute-start | bytes 3145736 | tf_op jit(solution)/shard_map/ppermute | solution.py:463
  19.3 9.0 %collective-permute-start.4 = (bf16[128,1024]{1,0:T(8,128)(2,1)S(1)}, bf16[128,1024]{1,0:T(8,128)(2,1)S(1)}, u32[]{:S(2)}, u32[]{:S(2)}) collective-permute-start(bf16[128,1024]{1,0:T(8,128)(2,1)S(1)} %pad_maximum_fusion.1), channel_id=1, source_target_pairs={{0,8},{8,0},{16,24},{24,16},{1,9},{9,1},{17,25},{25,17},{2,10},{10... | collective-permute-start | bytes 786440 | tf_op jit(solution)/shard_map/ppermute | solution.py:463
  19.9 8.5 %collective-permute-start.5 = (bf16[128,1024]{1,0:T(8,128)(2,1)S(1)}, bf16[128,1024]{1,0:T(8,128)(2,1)S(1)}, u32[]{:S(2)}, u32[]{:S(2)}) collective-permute-start(bf16[128,1024]{1,0:T(8,128)(2,1)S(1)} %pad_maximum_fusion.2), channel_id=1, source_target_pairs={{0,16},{8,24},{16,0},{24,8},{1,17},{9,25},{17,1},{25,9},{2,18},{10... | collective-permute-start | bytes 786440 | tf_op jit(solution)/shard_map/ppermute | solution.py:463
  30.0 2.8 %collective-permute-start.6 = (bf16[768,256]{1,0:T(8,128)(2,1)S(1)}, bf16[768,256]{1,0:T(8,128)(2,1)S(1)}, u32[]{:S(2)}, u32[]{:S(2)}) collective-permute-start(bf16[768,256]{1,0:T(8,128)(2,1)S(1)} %get-tuple-element.25), channel_id=1, source_target_pairs={{0,1},{1,0},{2,3},{3,2},{4,5},{5,4},{6,7},{7,6},{8,9},{9,8},{10,11... | collective-permute-start | bytes 1179656 | tf_op jit(solution)/shard_map/ppermute | solution.py:463
  30.1 6.9 %collective-permute-start.10 = (bf16[128,256]{1,0:T(8,128)(2,1)S(1)}, bf16[128,256]{1,0:T(8,128)(2,1)S(1)}, u32[]{:S(2)}, u32[]{:S(2)}) collective-permute-start(bf16[128,256]{1,0:T(8,128)(2,1)S(1)} %get-tuple-element.33), channel_id=1, source_target_pairs={{0,24},{8,16},{16,8},{24,0},{1,25},{9,17},{17,9},{25,1},{2,26},{10... | collective-permute-start | bytes 196616 | tf_op jit(solution)/shard_map/ppermute | solution.py:463
  33.4 6.3 %collective-permute-start.7 = (bf16[192,256]{1,0:T(8,128)(2,1)S(1)}, bf16[192,256]{1,0:T(8,128)(2,1)S(1)}, u32[]{:S(2)}, u32[]{:S(2)}) collective-permute-start(bf16[192,256]{1,0:T(8,128)(2,1)S(1)} %get-tuple-element.27), channel_id=1, source_target_pairs={{0,24},{1,25},{2,26},{3,27},{4,28},{5,29},{6,30},{7,31},{8,16},{9,... | collective-permute-start | bytes 294920 | tf_op jit(solution)/shard_map/ppermute | solution.py:485
  35.1 5.4 %collective-permute-start.8 = (bf16[192,256]{1,0:T(8,128)(2,1)S(1)}, bf16[192,256]{1,0:T(8,128)(2,1)S(1)}, u32[]{:S(2)}, u32[]{:S(2)}) collective-permute-start(bf16[192,256]{1,0:T(8,128)(2,1)S(1)} %get-tuple-element.28), channel_id=1, source_target_pairs={{0,8},{1,17},{2,10},{3,19},{4,12},{5,21},{6,14},{7,23},{8,0},{9,25... | collective-permute-start | bytes 294920 | tf_op jit(solution)/shard_map/ppermute | solution.py:485
  35.6 5.8 %collective-permute-start.9 = (bf16[192,256]{1,0:T(8,128)(2,1)S(1)}, bf16[192,256]{1,0:T(8,128)(2,1)S(1)}, u32[]{:S(2)}, u32[]{:S(2)}) collective-permute-start(bf16[192,256]{1,0:T(8,128)(2,1)S(1)} %get-tuple-element.29), channel_id=1, source_target_pairs={{0,16},{1,9},{2,18},{3,11},{4,20},{5,13},{6,22},{7,15},{8,24},{9,1... | collective-permute-start | bytes 294920 | tf_op jit(solution)/shard_map/ppermute | solution.py:485
  41.4 6.6 %collective-permute-start.11 = (bf16[320,256]{1,0:T(8,128)(2,1)S(1)}, bf16[320,256]{1,0:T(8,128)(2,1)S(1)}, u32[]{:S(2)}, u32[]{:S(2)}) collective-permute-start(bf16[320,256]{1,0:T(8,128)(2,1)S(1)} %pad_maximum_fusion.3), channel_id=1, source_target_pairs={{0,2},{1,5},{2,0},{3,7},{4,6},{5,1},{6,4},{7,3},{8,10},{9,13},{10,... | collective-permute-start | bytes 491528 | tf_op jit(solution)/shard_map/ppermute | solution.py:496
  48.1 6.6 %collective-permute-start.12 = (bf16[320,256]{1,0:T(8,128)(2,1)S(1)}, bf16[320,256]{1,0:T(8,128)(2,1)S(1)}, u32[]{:S(2)}, u32[]{:S(2)}) collective-permute-start(bf16[320,256]{1,0:T(8,128)(2,1)S(1)} %add_convert_fusion.2), channel_id=1, source_target_pairs={{0,4},{1,3},{2,6},{3,1},{4,0},{5,7},{6,2},{7,5},{8,12},{9,11},{10,... | collective-permute-start | bytes 491528 | tf_op jit(solution)/shard_map/ppermute | solution.py:496
  54.7 7.1 %collective-permute-start.15 = (bf16[320,256]{1,0:T(8,128)(2,1)S(1)}, bf16[320,256]{1,0:T(8,128)(2,1)S(1)}, u32[]{:S(2)}, u32[]{:S(2)}) collective-permute-start(bf16[320,256]{1,0:T(8,128)(2,1)S(1)} %add_convert_fusion.1), channel_id=1, source_target_pairs={{0,24},{1,25},{2,26},{3,27},{4,28},{5,29},{6,30},{7,31},{8,16},{9,... | collective-permute-start | bytes 491528 | tf_op jit(solution)/shard_map/ppermute | solution.py:485
  56.3 7.4 %collective-permute-start.16 = (bf16[320,256]{1,0:T(8,128)(2,1)S(1)}, bf16[320,256]{1,0:T(8,128)(2,1)S(1)}, u32[]{:S(2)}, u32[]{:S(2)}) collective-permute-start(bf16[320,256]{1,0:T(8,128)(2,1)S(1)} %add_convert_fusion.1), channel_id=1, source_target_pairs={{0,8},{1,17},{2,10},{3,19},{4,12},{5,21},{6,14},{7,23},{8,0},{9,25... | collective-permute-start | bytes 491528 | tf_op jit(solution)/shard_map/ppermute | solution.py:485
  56.3 7.5 %collective-permute-start.13 = (bf16[320,256]{1,0:T(8,128)(2,1)S(1)}, bf16[320,256]{1,0:T(8,128)(2,1)S(1)}, u32[]{:S(2)}, u32[]{:S(2)}) collective-permute-start(bf16[320,256]{1,0:T(8,128)(2,1)S(1)} %add_convert_fusion.1), channel_id=1, source_target_pairs={{0,16},{1,9},{2,18},{3,11},{4,20},{5,13},{6,22},{7,15},{8,24},{9,1... | collective-permute-start | bytes 491528 | tf_op jit(solution)/shard_map/ppermute | solution.py:485
  63.7 2.3 %collective-permute-start.17 = (bf16[640,256]{1,0:T(8,128)(2,1)S(1)}, bf16[640,256]{1,0:T(8,128)(2,1)S(1)}, u32[]{:S(2)}, u32[]{:S(2)}) collective-permute-start(bf16[640,256]{1,0:T(8,128)(2,1)S(1)} %constant_dynamic-update-slice_fusion.refs_1_), channel_id=1, source_target_pairs={{0,1},{1,0},{2,3},{3,2},{4,5},{5,4},{6,7},{7,6},{8,9},{9,8},{10,11... | collective-permute-start | bytes 983048 | tf_op jit(solution)/shard_map/ppermute | solution.py:463
  63.8 2.2 %collective-permute-start.14 = (bf16[640,256]{1,0:T(8,128)(2,1)S(1)}, bf16[640,256]{1,0:T(8,128)(2,1)S(1)}, u32[]{:S(2)}, u32[]{:S(2)}) collective-permute-start(bf16[640,256]{1,0:T(8,128)(2,1)S(1)} %pad_maximum_fusion.refs_0_), channel_id=1, source_target_pairs={{0,1},{1,0},{2,3},{3,2},{4,5},{5,4},{6,7},{7,6},{8,9},{9,8},{10,11... | collective-permute-start | bytes 983048 | tf_op jit(solution)/shard_map/ppermute | solution.py:463

commit v2 on v1

--- a/solution.py
+++ b/solution.py
@@ -76,13 +76,17 @@
     shift = q_rows.bit_length() - 1
     low = index & (q_rows - 1)
     one = jnp.left_shift(jnp.ones_like(index), (index >> shift) * 4)
-    spare = -terms % 8
-    low = jnp.concatenate([low, jnp.full((spare, 128), -1, jnp.int32)], axis=0)
-    one = jnp.concatenate([one, jnp.zeros((spare, 128), jnp.int32)], axis=0)
+    spare = -terms % 8 if -terms % 8 < 3 else 0
+    if spare == 0 and terms % 8:
+        turn = lambda array, by: jnp.concatenate([array[by:], array[:by]], axis=0)
+    else:
+        turn = lambda array, by: pltpu.roll(array, by, 0)
+    if spare:
+        low = jnp.concatenate([low, jnp.full((spare, 128), -1, jnp.int32)], axis=0)
+        one = jnp.concatenate([one, jnp.zeros((spare, 128), jnp.int32)], axis=0)
     unit = one
     for other in range(1, terms + spare):
-        same = pltpu.roll(low, other, 0) == low
-        unit = unit + jnp.where(same, pltpu.roll(one, other, 0), jnp.zeros_like(one))
+        unit = unit + jnp.where(turn(low, other) == low, turn(one, other), jnp.zeros_like(one))
     tall = min(256, q_rows) // TILE
     shape = (tall, TILE, 128)
     place = lax.broadcasted_iota(jnp.int32, shape, 0) * TILE + lax.broadcasted_iota(jnp.int32, shape, 1)
@@ -100,13 +104,15 @@
         store(top, tall, word)
 
 
-def unpack(word_ref, field, lanes, count_ref):
-    words = word_ref[:, :, lanes]
+def unpack(word_ref, field, lanes, count_ref, part=0, parts=1):
+    deep = word_ref.shape[0] // parts
+    words = word_ref[part * deep : (part + 1) * deep, :, lanes]
     if field < FIELDS - 1:
         counts = words & (15 << (4 * field))
     else:
         counts = (words >> (4 * field)) & 15
-    count_ref[...] = counts.astype(BF16).reshape(count_ref.shape)
+    rows = slice(part * deep * TILE, (part + 1) * deep * TILE)
+    count_ref[rows, :] = counts.astype(BF16).reshape(deep * TILE, count_ref.shape[1])
 
 
 def unpacked_scale(field):
@@ -220,15 +226,21 @@
     row_grad_ref[...] = row_grad_in[...]
     index_ref[...] = index_in[...]
     tall, rows = counts[0].shape
-    tiles = rows // 128 // 2 // FIELDS
+    tiles = rows // 128 // 2 // FIELDS // 2
+    wide = row_grad_ref.shape[1] // 2
     unpack(word_ref, 0, slice(None), counts[0])
     for field in range(FIELDS):
-        found = jnp.dot(counts[field % 2][...], row_grad_ref[...], preferred_element_type=F32)
-        found = found * (scale / unpacked_scale(field))
-        sums_ref[field * tall : (field + 1) * tall, :] = found.astype(BF16)
-        if field + 1 < FIELDS:
-            unpack(word_ref, field + 1, slice(None), counts[(field + 1) % 2])
-        build_tiles(index_ref, cold_word_ref, field * tiles, tiles, field * tiles)
+        for part in range(2):
+            lanes = slice(part * wide, (part + 1) * wide)
+            found = jnp.dot(
+                counts[field % 2][...], row_grad_ref[:, lanes], preferred_element_type=F32
+            )
+            found = found * (scale / unpacked_scale(field))
+            sums_ref[field * tall : (field + 1) * tall, lanes] = found.astype(BF16)
+            if field + 1 < FIELDS:
+                unpack(word_ref, field + 1, slice(None), counts[(field + 1) % 2], part, 2)
+            first = (2 * field + part) * tiles
+            build_tiles(index_ref, cold_word_ref, first, tiles, first)
     send_ref[...] = sums_ref[: 2 * tall, :]
     keep_ref[...] = sums_ref[2 * tall :, :]
     cold_word_out[...] = cold_word_ref[...]
@@ -272,34 +284,41 @@
     word_ref[:, :, :half] = word_in[...]
     index_ref[...] = index_in[...]
     row_grad_ref[...] = row_grad_in[...]
-    tiles = half // 128 // FIELDS
-
-    def add_product(field):
-        rows = slice(field * tall, (field + 1) * tall)
-        part = transposed_dot(held_ref[rows, :], sums_ref[rows, :])
-        grad_ref[...] = part if field == 0 else grad_ref[...] + part
+    tiles = half // 128 // FIELDS // 2
+    wide, deep = row_grad_ref.shape[1] // 2, held_ref.shape[1] // 2
+
+    def add_product(field, part):
+        rows, lanes = slice(field * tall, (field + 1) * tall), slice(part * deep, (part + 1) * deep)
+        found = transposed_dot(held_ref[rows, lanes], sums_ref[rows, :])
+        grad_ref[lanes, :] = found if field == 0 else grad_ref[lanes, :] + found
 
     steps = [(k, field) for k in range(2) for field in range(FIELDS)]
     unpack(word_ref, 0, slice(half), counts[0])
     for step, (k, field) in enumerate(steps):
+        if step == FIELDS + 1:
+            fetch.wait()
         depth, rows = slice(k * half, (k + 1) * half), slice(field * tall, (field + 1) * tall)
-        found = jnp.dot(counts[step % 2][...], row_grad_ref[depth, :], preferred_element_type=F32)
-        if k == 0:
-            part_ref[rows, :] = found
-            first = half // 128 + field * tiles
-            build_tiles(index_ref, word_ref, first, tiles, first)
-        else:
-            found = (part_ref[rows, :] + found) * (scale / unpacked_scale(field))
-            sums_ref[rows, :] = found.astype(BF16)
-        if step + 1 < len(steps):
-            ahead, next_field = steps[step + 1]
-            lanes = slice(ahead * half, (ahead + 1) * half)
-            unpack(word_ref, next_field, lanes, counts[(step + 1) % 2])
-        if k == 1 and field == 0:
-            fetch.wait()
-        if k == 1 and field > 0:
-            add_product(field - 1)
-    add_product(FIELDS - 1)
+        for part in range(2):
+            lanes = slice(part * wide, (part + 1) * wide)
+            found = jnp.dot(
+                counts[step % 2][...], row_grad_ref[depth, lanes], preferred_element_type=F32
+            )
+            if k == 0:
+                part_ref[rows, lanes] = found
+                first = half // 128 + (2 * field + part) * tiles
+                build_tiles(index_ref, word_ref, first, tiles, first)
+            else:
+                found = (part_ref[rows, lanes] + found) * (scale / unpacked_scale(field))
+                sums_ref[rows, lanes] = found.astype(BF16)
+            if step + 1 < len(steps) and (step + 1 != FIELDS or part == 1):
+                ahead, next_field = steps[step + 1]
+                there = slice(ahead * half, (ahead + 1) * half)
+                at = (0, 1) if step + 1 == FIELDS else (part, 2)
+                unpack(word_ref, next_field, there, counts[(step + 1) % 2], *at)
+            if k == 1 and field > 0:
+                add_product(field - 1, part)
+    for part in range(2):
+        add_product(FIELDS - 1, part)
     grad_out[...] = grad_ref[...]
 
 
@@ -331,7 +350,7 @@
 
 
 def join_kernel(parts, place_ref, cold_ref, keep_ref, other_ref, *rest):
-    feats, (own_ref, send_ref, sums_ref, held_ref, total_ref) = rest[:parts], rest[parts:]
+    feats, (own_ref, send_ref, sums_ref, held_ref, total_ref) = rest[:parts], rest[-5:]
     d_in, wide = own_ref.shape
     sums = keep_ref[...].astype(F32) + other_ref[...].astype(F32)
     sums_ref[...] = sums.astype(BF16)
@@ -362,12 +381,12 @@
         send_ref[rows, :] = first
 
 
-def join(place, cold, keep, other, feats):
+def join(place, cold, keep, other, feats, arrived):
     d_in, d_h = cold.shape
     half = jax.ShapeDtypeStruct((d_in, d_h // 2), BF16)
     return pl.pallas_call(
         functools.partial(join_kernel, len(feats)),
-        in_specs=[scalars()] + [whole()] * (3 + len(feats)),
+        in_specs=[scalars()] + [whole()] * (3 + len(feats)) + [in_place()],
         out_specs=[whole()] * 2,
         out_shape=[half, half],
         scratch_shapes=[
@@ -378,7 +397,7 @@
         compiler_params=params(32),
         cost_estimate=cost(2 * keep.shape[0] * d_h * d_in, 4 * d_in * d_h),
         name="join",
-    )(place, cold, keep, other, *feats)
+    )(place, cold, keep, other, *feats, arrived)
 
 
 def share_rows(rows, members, place_ref, core, turn):
@@ -534,7 +553,7 @@
     send, keep, words = hot_sums(words, row_grad, cold_index.T, cold_rows, fanout)
     other = exchange(send, "copy", 1)
     cold = cold_grad(words, cold_index.T, row_grad, cold_feats, fanout)
-    own_one, twin_one = join(place, cold, keep, other, feats)
+    own_one, twin_one = join(place, cold, keep, other, feats, two)
     shares = pair_sums(place, own_one, exchange(twin_one, "copy", 1), n_clique)
     shares = sum_over_slice(shares, two)
     middle = n_clique // 2

time: 68.2 us -> 69.1 us (1.013)
  starting transfers between devices: 20.3 us -> 22.9 us
  waiting for transfers between devices: 19.3 us -> 17.9 us
    ppermute x2, waiting for transfers between devices: 9.54 us -> 7.4 us  [sum_over_slice(): own = added(own, lax.ppermute(own, 'copy', route))]
    ppermute x6, starting transfers between devices: 7.11 us -> 9.08 us  [trade(): lax.ppermute(arrays[turn], ('clique', 'copy'), route_of(n_clique, n_copy,...]
    ppermute x10, waiting for transfers between devices: 0.03 us -> 1.73 us  [exchange(): lax.ppermute(array, axis, [(source, source ^ step) for source in range(si...]
    ppermute x2, starting transfers between devices: 3.66 us -> 4.75 us  [sum_over_slice(): own = added(own, lax.ppermute(own, 'copy', route))]
    ppermute x6, waiting for transfers between devices: 9.77 us -> 8.81 us  [trade(): lax.ppermute(arrays[turn], ('clique', 'copy'), route_of(n_clique, n_copy,...]
  transfers between devices with their start and end apart: 18 -> 18, of which waited for: 7 -> 8; matrix products, arithmetic and copies ran while one was open for 0% -> 0% of each run, Pallas kernels for 31% -> 30%
where the time goes in v2:
time: 69.1 us
  Pallas kernels  24.9 us (36%)
  starting transfers between devices  22.9 us (33%)
  waiting for transfers between devices  17.9 us (26%)
  between operations  1.74 us (3%)
  local copies, waits for them, and re-layouts  1.23 us (2%)
    ppermute x6, starting transfers between devices, trade(): lax.ppermute(arrays[turn], ('clique', 'copy'), route_of(n_clique, n_copy,...  9.08 us
    ppermute x10, starting transfers between devices, exchange(): lax.ppermute(array, axis, [(source, source ^ step) for source in range(si...  9.03 us
    ppermute x6, waiting for transfers between devices, trade(): lax.ppermute(arrays[turn], ('clique', 'copy'), route_of(n_clique, n_copy,...  8.81 us
    pallas_call x1, Pallas kernels, cold_grad(): pl.pallas_call(functools.partial(cold_kernel, 1.0 / fanout), in_specs=[wh...  8 us
    ppermute x2, waiting for transfers between devices, sum_over_slice(): own = added(own, lax.ppermute(own, 'copy', route))  7.4 us
    pallas_call x1, Pallas kernels, hot_sums(): pl.pallas_call(functools.partial(hot_kernel, 1.0 / fanout), in_specs=[who...  5.88 us
    pallas_call x1, Pallas kernels, row_gradients(): pl.pallas_call(functools.partial(rows_kernel, shard_rows.bit_length() - 1...  4.84 us
    ppermute x2, starting transfers between devices, sum_over_slice(): own = added(own, lax.ppermute(own, 'copy', route))  4.75 us
  transfers between devices with their start and end apart: 18, of which 8 were waited for; matrix products, arithmetic and copies ran while one was open for 0% of the time, Pallas kernels for 30%

profile of v2, /device:TPU:0, one launch (start us, length us, event | category | flops | bytes accessed | tf_op | source)
XLA Modules:
  0.0 69.1 jit_solution(15153382695314404156)
XLA Ops:
  0.6 0.1 pad_add_fusion.place_ref
  0.7 1.1 %copy-done.3 = bf16[512,768]{1,0:T(8,128)(2,1)S(1)} copy-done((bf16[512,768]{1,0:T(8,128)(2,1)S(1)}, bf16[512,768]{1,0:T(8,128)(2,1)}, u32[]{:S(2)}) %copy-start.3) | copy-done | bytes 786456
  1.9 0.6 half_of.1.rest_0_
  2.4 3.0 %collective-permute-start.2 = (bf16[256,768]{1,0:T(8,128)(2,1)S(1)}, bf16[256,768]{1,0:T(8,128)(2,1)S(1)}, u32[]{:S(2)}, u32[]{:S(2)}) collective-permute-start(bf16[256,768]{1,0:T(8,128)(2,1)S(1)} %half_of.1.rest_0_), channel_id=1, source_target_pairs={{0,16},{8,24},{16,0},{24,8},{1,17},{9,25},{17,1},{25,9},{2,18},{10... | collective-permute-start | bytes 1179656 | tf_op jit(solution)/shard_map/ppermute | solution.py:482
  5.5 1.5 %collective-permute-start.1 = (bf16[256,768]{1,0:T(8,128)(2,1)S(1)}, bf16[256,768]{1,0:T(8,128)(2,1)S(1)}, u32[]{:S(2)}, u32[]{:S(2)}) collective-permute-start(bf16[256,768]{1,0:T(8,128)(2,1)S(1)} %half_of.1.rest_0_), channel_id=1, source_target_pairs={{0,8},{8,0},{16,24},{24,16},{1,9},{9,1},{17,25},{25,17},{2,10},{10... | collective-permute-start | bytes 1179656 | tf_op jit(solution)/shard_map/ppermute | solution.py:482
  7.7 0.0 copy-start.6
  7.7 4.8 %row_gradients.1 = (bf16[2048,512]{1,0:T(8,128)(2,1)S(1)}, bf16[512,256]{1,0:T(8,128)(2,1)S(1)}, bf16[512,256]{1,0:T(8,128)(2,1)S(1)}, s16[32,16,2048]{2,1,0:T(8,128)(2,1)S(1)}) custom-call(s32[2]{0:T(128)S(1)} %pad_add_fusion.place_ref, s32[1]{0:T(128)S(6)} %copy.15.count_ref, s32[10,2048]{1,0:T(8,128)S(1)} %bitcast.4, bf16[2048,512]{1,0:T(8,128)(2,1)S(1)} %copy-done.1, ...), custom_call_target="tpu_custom_call" | custom-call | flops 10000000000 | bytes 100000000 | tf_op jit(solution)/shard_map/row_gradients/pallas_call | solution.py:184
  12.5 0.1 collective-permute-start.3
  12.6 0.0 copy-start
  12.6 5.9 %hot_sums.1 = (bf16[1024,512]{1,0:T(8,128)(2,1)S(1)}, bf16[1024,512]{1,0:T(8,128)(2,1)S(1)}, s16[32,16,1024]{2,1,0:T(8,128)(2,1)S(1)}) custom-call(s16[32,16,2048]{2,1,0:T(8,128)(2,1)S(1)} %get-tuple-element.17.word_in, bf16[2048,512]{1,0:T(8,128)(2,1)S(1)} %get-tuple-element.18.row_grad_in, s32[15,2048]{1,0:T(8,128)S(1)} %bitcast.5), custom_call_target="tpu_custom_call" | custom-call | flops 10000000000 | bytes 100000000 | tf_op jit(solution)/shard_map/hot_sums/pallas_call | solution.py:253
  18.5 0.5 collective-permute-start
  19.0 0.0 collective-permute-done.3
  19.1 0.1 add_convert_fusion
  19.1 0.4 collective-permute-start.6
  19.5 0.0 collective-permute-done.1.rest_1_
  19.6 1.7 %collective-permute-start.5 = (bf16[128,1024]{1,0:T(8,128)(2,1)S(1)}, bf16[128,1024]{1,0:T(8,128)(2,1)S(1)}, u32[]{:S(2)}, u32[]{:S(2)}) collective-permute-start(bf16[128,1024]{1,0:T(8,128)(2,1)S(1)} %pad_maximum_fusion.2), channel_id=1, source_target_pairs={{0,16},{8,24},{16,0},{24,8},{1,17},{9,25},{17,1},{25,9},{2,18},{10... | collective-permute-start | bytes 786440 | tf_op jit(solution)/shard_map/ppermute | solution.py:482
  21.3 0.0 collective-permute-done.2.rest_2_
  21.4 1.6 %collective-permute-start.4 = (bf16[128,1024]{1,0:T(8,128)(2,1)S(1)}, bf16[128,1024]{1,0:T(8,128)(2,1)S(1)}, u32[]{:S(2)}, u32[]{:S(2)}) collective-permute-start(bf16[128,1024]{1,0:T(8,128)(2,1)S(1)} %pad_maximum_fusion.1), channel_id=1, source_target_pairs={{0,8},{8,0},{16,24},{24,16},{1,9},{9,1},{17,25},{25,17},{2,10},{10... | collective-permute-start | bytes 786440 | tf_op jit(solution)/shard_map/ppermute | solution.py:482
  22.9 8.0 %cold_grad.1.cold_ref = f32[768,512]{1,0:T(8,128)S(1)} custom-call(s16[32,16,1024]{2,1,0:T(8,128)(2,1)S(1)} %get-tuple-element.19.word_in, s32[15,2048]{1,0:T(8,128)S(1)} %bitcast.6, bf16[2048,512]{1,0:T(8,128)(2,1)S(1)} %get-tuple-element.18.row_grad_in, bf16[2048,768]{1,0:T(8,128)(2,1)S(1)} %copy-done), custom_call_target="tpu_custom_call" | custom-call | flops 10000000000 | bytes 100000000 | tf_op jit(solution)/shard_map/cold_grad/pallas_call | solution.py:329
  30.9 0.0 collective-permute-done.6
  30.9 0.0 collective-permute-done.5.rest_4_
  31.0 0.0 collective-permute-done.4.rest_3_
  31.0 1.6 %join.1 = (bf16[768,256]{1,0:T(8,128)(2,1)S(1)}, bf16[768,256]{1,0:T(8,128)(2,1)S(1)}) custom-call(s32[2]{0:T(128)S(1)} %pad_add_fusion.place_ref, f32[768,512]{1,0:T(8,128)S(1)} %cold_grad.1.cold_ref, bf16[1024,512]{1,0:T(8,128)(2,1)S(1)} %get-tuple-element.20.keep_ref, bf16[1024,512]{1,0:T(8,128)(2,1)S(1)} %collective-permute-done.other_ref, ...), custom_call_target="tpu_custom_call" | custom-call | flops 805306368 | bytes 1572864 | tf_op jit(solution)/shard_map/join/pallas_call | solution.py:387
  32.7 0.1 collective-permute-start.7
  32.7 1.7 %collective-permute-done.7.other_ref = bf16[768,256]{1,0:T(8,128)(2,1)S(1)} collective-permute-done((bf16[768,256]{1,0:T(8,128)(2,1)S(1)}, bf16[768,256]{1,0:T(8,128)(2,1)S(1)}, u32[]{:S(2)}, u32[]{:S(2)}) %collective-permute-start.7) | collective-permute-done | bytes 393248 | tf_op jit(solution)/shard_map/ppermute | solution.py:482
  34.5 0.6 pair_sums.1
  35.1 0.4 collective-permute-start.8
  35.5 1.7 %collective-permute-start.9 = (bf16[192,256]{1,0:T(8,128)(2,1)S(1)}, bf16[192,256]{1,0:T(8,128)(2,1)S(1)}, u32[]{:S(2)}, u32[]{:S(2)}) collective-permute-start(bf16[192,256]{1,0:T(8,128)(2,1)S(1)} %get-tuple-element.28), channel_id=1, source_target_pairs={{0,8},{1,17},{2,10},{3,19},{4,12},{5,21},{6,14},{7,23},{8,0},{9,25... | collective-permute-start | bytes 294920 | tf_op jit(solution)/shard_map/ppermute | solution.py:504
  37.2 1.5 %collective-permute-start.10 = (bf16[192,256]{1,0:T(8,128)(2,1)S(1)}, bf16[192,256]{1,0:T(8,128)(2,1)S(1)}, u32[]{:S(2)}, u32[]{:S(2)}) collective-permute-start(bf16[192,256]{1,0:T(8,128)(2,1)S(1)} %get-tuple-element.29), channel_id=1, source_target_pairs={{0,16},{1,9},{2,18},{3,11},{4,20},{5,13},{6,22},{7,15},{8,24},{9,1... | collective-permute-start | bytes 294920 | tf_op jit(solution)/shard_map/ppermute | solution.py:504
  38.7 3.1 %collective-permute-done.8 = bf16[192,256]{1,0:T(8,128)(2,1)S(1)} collective-permute-done((bf16[192,256]{1,0:T(8,128)(2,1)S(1)}, bf16[192,256]{1,0:T(8,128)(2,1)S(1)}, u32[]{:S(2)}, u32[]{:S(2)}) %collective-permute-start.8) | collective-permute-done | bytes 98336 | tf_op jit(solution)/shard_map/ppermute | solution.py:504
  41.8 0.3 collective-permute-done.9
  42.1 0.2 collective-permute-done.10
  42.3 0.1 add_convert_fusion.3
  42.4 1.7 %collective-permute-start.11 = (bf16[320,256]{1,0:T(8,128)(2,1)S(1)}, bf16[320,256]{1,0:T(8,128)(2,1)S(1)}, u32[]{:S(2)}, u32[]{:S(2)}) collective-permute-start(bf16[320,256]{1,0:T(8,128)(2,1)S(1)} %pad_maximum_fusion.3), channel_id=1, source_target_pairs={{0,2},{1,5},{2,0},{3,7},{4,6},{5,1},{6,4},{7,3},{8,10},{9,13},{10,... | collective-permute-start | bytes 491528 | tf_op jit(solution)/shard_map/ppermute | solution.py:515
  44.0 4.0 %collective-permute-done.11 = bf16[320,256]{1,0:T(8,128)(2,1)S(1)} collective-permute-done((bf16[320,256]{1,0:T(8,128)(2,1)S(1)}, bf16[320,256]{1,0:T(8,128)(2,1)S(1)}, u32[]{:S(2)}, u32[]{:S(2)}) %collective-permute-start.11) | collective-permute-done | bytes 163872 | tf_op jit(solution)/shard_map/ppermute | solution.py:515
  48.1 3.1 %collective-permute-start.12 = (bf16[320,256]{1,0:T(8,128)(2,1)S(1)}, bf16[320,256]{1,0:T(8,128)(2,1)S(1)}, u32[]{:S(2)}, u32[]{:S(2)}) collective-permute-start(bf16[320,256]{1,0:T(8,128)(2,1)S(1)} %add_convert_fusion.2), channel_id=1, source_target_pairs={{0,4},{1,3},{2,6},{3,1},{4,0},{5,7},{6,2},{7,5},{8,12},{9,11},{10,... | collective-permute-start | bytes 491528 | tf_op jit(solution)/shard_map/ppermute | solution.py:515
  51.2 3.4 %collective-permute-done.12 = bf16[320,256]{1,0:T(8,128)(2,1)S(1)} collective-permute-done((bf16[320,256]{1,0:T(8,128)(2,1)S(1)}, bf16[320,256]{1,0:T(8,128)(2,1)S(1)}, u32[]{:S(2)}, u32[]{:S(2)}) %collective-permute-start.12) | collective-permute-done | bytes 163872 | tf_op jit(solution)/shard_map/ppermute | solution.py:515
  54.6 1.4 %collective-permute-start.13 = (bf16[320,256]{1,0:T(8,128)(2,1)S(1)}, bf16[320,256]{1,0:T(8,128)(2,1)S(1)}, u32[]{:S(2)}, u32[]{:S(2)}) collective-permute-start(bf16[320,256]{1,0:T(8,128)(2,1)S(1)} %add_convert_fusion.1), channel_id=1, source_target_pairs={{0,16},{1,9},{2,18},{3,11},{4,20},{5,13},{6,22},{7,15},{8,24},{9,1... | collective-permute-start | bytes 491528 | tf_op jit(solution)/shard_map/ppermute | solution.py:504
  56.0 4.1 %collective-permute-start.15 = (bf16[320,256]{1,0:T(8,128)(2,1)S(1)}, bf16[320,256]{1,0:T(8,128)(2,1)S(1)}, u32[]{:S(2)}, u32[]{:S(2)}) collective-permute-start(bf16[320,256]{1,0:T(8,128)(2,1)S(1)} %add_convert_fusion.1), channel_id=1, source_target_pairs={{0,24},{1,25},{2,26},{3,27},{4,28},{5,29},{6,30},{7,31},{8,16},{9,... | collective-permute-start | bytes 491528 | tf_op jit(solution)/shard_map/ppermute | solution.py:504
  60.1 0.0 collective-permute-start.16
  60.1 3.8 %collective-permute-done.13 = bf16[320,256]{1,0:T(8,128)(2,1)S(1)} collective-permute-done((bf16[320,256]{1,0:T(8,128)(2,1)S(1)}, bf16[320,256]{1,0:T(8,128)(2,1)S(1)}, u32[]{:S(2)}, u32[]{:S(2)}) %collective-permute-start.13) | collective-permute-done | bytes 163872 | tf_op jit(solution)/shard_map/ppermute | solution.py:504
  64.0 0.1 collective-permute-start.14
  64.0 0.0 collective-permute-done.15
  64.1 1.4 %collective-permute-done.16 = bf16[320,256]{1,0:T(8,128)(2,1)S(1)} collective-permute-done((bf16[320,256]{1,0:T(8,128)(2,1)S(1)}, bf16[320,256]{1,0:T(8,128)(2,1)S(1)}, u32[]{:S(2)}, u32[]{:S(2)}) %collective-permute-start.16) | collective-permute-done | bytes 163872 | tf_op jit(solution)/shard_map/ppermute | solution.py:504
  65.5 0.1 collective-permute-start.17
  65.6 1.7 %lay.2 = (f32[768,512]{1,0:T(8,128)}, f32[512,512]{1,0:T(8,128)}) custom-call(s32[2]{0:T(128)S(1)} %pad_add_fusion.place_ref, bf16[640,256]{1,0:T(8,128)(2,1)S(1)} %pad_maximum_fusion.refs_0_, bf16[640,256]{1,0:T(8,128)(2,1)S(1)} %constant_dynamic-update-slice_fusion.refs_1_), custom_call_target="tpu_custom_call" | custom-call | flops 10000000000 | bytes 100000000 | tf_op jit(solution)/shard_map/lay/pallas_call | solution.py:466
  67.2 0.0 collective-permute-done.14.refs_0_
  67.2 1.7 %lay.3 = (f32[768,512]{1,0:T(8,128)}, f32[512,512]{1,0:T(8,128)}) custom-call(s32[2]{0:T(128)S(1)} %pad_add_fusion.place_ref, bf16[640,256]{1,0:T(8,128)(2,1)S(1)} %collective-permute-done.14.refs_0_, bf16[640,256]{1,0:T(8,128)(2,1)S(1)} %collective-permute-done.17.refs_1_, ...), custom_call_target="tpu_custom_call", output_to_operand_aliasing={{0}: (3, {}), {1}: (4, {})} | custom-call | flops 10000000000 | bytes 100000000 | tf_op jit(solution)/shard_map/lay/pallas_call | solution.py:466
  (25 shorter events, 0.3 us)
Async XLA Ops:
  0.7 1.1 %copy-start.3 = (bf16[512,768]{1,0:T(8,128)(2,1)S(1)}, bf16[512,768]{1,0:T(8,128)(2,1)}, u32[]{:S(2)}) copy-start(bf16[512,768]{1,0:T(8,128)(2,1)} %feats_ref.3) | copy-start | bytes 2359300
  1.8 5.8 %copy-start.1 = (bf16[2048,512]{1,0:T(8,128)(2,1)S(1)}, bf16[2048,512]{1,0:T(8,128)(2,1)}, u32[]{:S(2)}) copy-start(bf16[2048,512]{1,0:T(8,128)(2,1)} %out_grad_ref.1) | copy-start | bytes 6291460
  1.8 5.8 %copy-start.2 = (bf16[2048,512]{1,0:T(8,128)(2,1)S(1)}, bf16[2048,512]{1,0:T(8,128)(2,1)}, u32[]{:S(2)}) copy-start(bf16[2048,512]{1,0:T(8,128)(2,1)} %pre_act_ref.1) | copy-start | bytes 6291460
  1.8 5.8 %copy-start.4 = (bf16[512,512]{1,0:T(8,128)(2,1)S(1)}, bf16[512,512]{1,0:T(8,128)(2,1)}, u32[]{:S(2)}) copy-start(bf16[512,512]{1,0:T(8,128)(2,1)} %layer_two_ref.1) | copy-start | bytes 1572868
  1.9 5.8 %copy-start.5 = (s32[2048,10]{0,1:T(8,128)S(1)}, s32[2048,10]{0,1:T(8,128)}, u32[]{:S(2)}) copy-start(s32[2048,10]{0,1:T(8,128)} %param.12) | copy-start | bytes 245764
  2.4 18.9 %collective-permute-start.2 = (bf16[256,768]{1,0:T(8,128)(2,1)S(1)}, bf16[256,768]{1,0:T(8,128)(2,1)S(1)}, u32[]{:S(2)}, u32[]{:S(2)}) collective-permute-start(bf16[256,768]{1,0:T(8,128)(2,1)S(1)} %half_of.1.rest_0_), channel_id=1, source_target_pairs={{0,16},{8,24},{16,0},{24,8},{1,17},{9,25},{17,1},{25,9},{2,18},{10... | collective-permute-start | bytes 1179656 | tf_op jit(solution)/shard_map/ppermute | solution.py:482
  5.5 14.1 %collective-permute-start.1 = (bf16[256,768]{1,0:T(8,128)(2,1)S(1)}, bf16[256,768]{1,0:T(8,128)(2,1)S(1)}, u32[]{:S(2)}, u32[]{:S(2)}) collective-permute-start(bf16[256,768]{1,0:T(8,128)(2,1)S(1)} %half_of.1.rest_0_), channel_id=1, source_target_pairs={{0,8},{8,0},{16,24},{24,16},{1,9},{9,1},{17,25},{25,17},{2,10},{10... | collective-permute-start | bytes 1179656 | tf_op jit(solution)/shard_map/ppermute | solution.py:482
  7.7 4.9 %copy-start.6 = (s32[2048,15]{0,1:T(8,128)S(1)}, s32[2048,15]{0,1:T(8,128)}, u32[]{:S(2)}) copy-start(s32[2048,15]{0,1:T(8,128)} %param.13) | copy-start | bytes 368644
  12.5 6.5 %collective-permute-start.3 = (bf16[512,256]{1,0:T(8,128)(2,1)S(1)}, bf16[512,256]{1,0:T(8,128)(2,1)S(1)}, u32[]{:S(2)}, u32[]{:S(2)}) collective-permute-start(bf16[512,256]{1,0:T(8,128)(2,1)S(1)} %get-tuple-element.23), channel_id=1, source_target_pairs={{0,1},{1,0},{2,3},{3,2},{4,5},{5,4},{6,7},{7,6},{8,9},{9,8},{10,11... | collective-permute-start | bytes 786440 | tf_op jit(solution)/shard_map/ppermute | solution.py:482
  12.6 10.3 %copy-start = (bf16[2048,768]{1,0:T(8,128)(2,1)S(1)}, bf16[2048,768]{1,0:T(8,128)(2,1)}, u32[]{:S(2)}) copy-start(bf16[2048,768]{1,0:T(8,128)(2,1)} %feats_ref.2) | copy-start | bytes 9437188
  18.5 12.5 %collective-permute-start = (bf16[1024,512]{1,0:T(8,128)(2,1)S(1)}, bf16[1024,512]{1,0:T(8,128)(2,1)S(1)}, u32[]{:S(2)}, u32[]{:S(2)}) collective-permute-start(bf16[1024,512]{1,0:T(8,128)(2,1)S(1)} %get-tuple-element.21), channel_id=1, source_target_pairs={{0,1},{1,0},{2,3},{3,2},{4,5},{5,4},{6,7},{7,6},{8,9},{9,8},{10,11... | collective-permute-start | bytes 3145736 | tf_op jit(solution)/shard_map/ppermute | solution.py:482
  19.1 11.8 %collective-permute-start.6 = (bf16[128,256]{1,0:T(8,128)(2,1)S(1)}, bf16[128,256]{1,0:T(8,128)(2,1)S(1)}, u32[]{:S(2)}, u32[]{:S(2)}) collective-permute-start(bf16[128,256]{1,0:T(8,128)(2,1)S(1)} %get-tuple-element.33), channel_id=1, source_target_pairs={{0,24},{8,16},{16,8},{24,0},{1,25},{9,17},{17,9},{25,1},{2,26},{10... | collective-permute-start | bytes 196616 | tf_op jit(solution)/shard_map/ppermute | solution.py:482
  19.6 11.4 %collective-permute-start.5 = (bf16[128,1024]{1,0:T(8,128)(2,1)S(1)}, bf16[128,1024]{1,0:T(8,128)(2,1)S(1)}, u32[]{:S(2)}, u32[]{:S(2)}) collective-permute-start(bf16[128,1024]{1,0:T(8,128)(2,1)S(1)} %pad_maximum_fusion.2), channel_id=1, source_target_pairs={{0,16},{8,24},{16,0},{24,8},{1,17},{9,25},{17,1},{25,9},{2,18},{10... | collective-permute-start | bytes 786440 | tf_op jit(solution)/shard_map/ppermute | solution.py:482
  21.4 9.6 %collective-permute-start.4 = (bf16[128,1024]{1,0:T(8,128)(2,1)S(1)}, bf16[128,1024]{1,0:T(8,128)(2,1)S(1)}, u32[]{:S(2)}, u32[]{:S(2)}) collective-permute-start(bf16[128,1024]{1,0:T(8,128)(2,1)S(1)} %pad_maximum_fusion.1), channel_id=1, source_target_pairs={{0,8},{8,0},{16,24},{24,16},{1,9},{9,1},{17,25},{25,17},{2,10},{10... | collective-permute-start | bytes 786440 | tf_op jit(solution)/shard_map/ppermute | solution.py:482
  32.7 1.8 %collective-permute-start.7 = (bf16[768,256]{1,0:T(8,128)(2,1)S(1)}, bf16[768,256]{1,0:T(8,128)(2,1)S(1)}, u32[]{:S(2)}, u32[]{:S(2)}) collective-permute-start(bf16[768,256]{1,0:T(8,128)(2,1)S(1)} %get-tuple-element.25), channel_id=1, source_target_pairs={{0,1},{1,0},{2,3},{3,2},{4,5},{5,4},{6,7},{7,6},{8,9},{9,8},{10,11... | collective-permute-start | bytes 1179656 | tf_op jit(solution)/shard_map/ppermute | solution.py:482
  35.1 6.6 %collective-permute-start.8 = (bf16[192,256]{1,0:T(8,128)(2,1)S(1)}, bf16[192,256]{1,0:T(8,128)(2,1)S(1)}, u32[]{:S(2)}, u32[]{:S(2)}) collective-permute-start(bf16[192,256]{1,0:T(8,128)(2,1)S(1)} %get-tuple-element.27), channel_id=1, source_target_pairs={{0,24},{1,25},{2,26},{3,27},{4,28},{5,29},{6,30},{7,31},{8,16},{9,... | collective-permute-start | bytes 294920 | tf_op jit(solution)/shard_map/ppermute | solution.py:504
  35.5 6.6 %collective-permute-start.9 = (bf16[192,256]{1,0:T(8,128)(2,1)S(1)}, bf16[192,256]{1,0:T(8,128)(2,1)S(1)}, u32[]{:S(2)}, u32[]{:S(2)}) collective-permute-start(bf16[192,256]{1,0:T(8,128)(2,1)S(1)} %get-tuple-element.28), channel_id=1, source_target_pairs={{0,8},{1,17},{2,10},{3,19},{4,12},{5,21},{6,14},{7,23},{8,0},{9,25... | collective-permute-start | bytes 294920 | tf_op jit(solution)/shard_map/ppermute | solution.py:504
  37.2 5.1 %collective-permute-start.10 = (bf16[192,256]{1,0:T(8,128)(2,1)S(1)}, bf16[192,256]{1,0:T(8,128)(2,1)S(1)}, u32[]{:S(2)}, u32[]{:S(2)}) collective-permute-start(bf16[192,256]{1,0:T(8,128)(2,1)S(1)} %get-tuple-element.29), channel_id=1, source_target_pairs={{0,16},{1,9},{2,18},{3,11},{4,20},{5,13},{6,22},{7,15},{8,24},{9,1... | collective-permute-start | bytes 294920 | tf_op jit(solution)/shard_map/ppermute | solution.py:504
  42.4 5.7 %collective-permute-start.11 = (bf16[320,256]{1,0:T(8,128)(2,1)S(1)}, bf16[320,256]{1,0:T(8,128)(2,1)S(1)}, u32[]{:S(2)}, u32[]{:S(2)}) collective-permute-start(bf16[320,256]{1,0:T(8,128)(2,1)S(1)} %pad_maximum_fusion.3), channel_id=1, source_target_pairs={{0,2},{1,5},{2,0},{3,7},{4,6},{5,1},{6,4},{7,3},{8,10},{9,13},{10,... | collective-permute-start | bytes 491528 | tf_op jit(solution)/shard_map/ppermute | solution.py:515
  48.1 6.5 %collective-permute-start.12 = (bf16[320,256]{1,0:T(8,128)(2,1)S(1)}, bf16[320,256]{1,0:T(8,128)(2,1)S(1)}, u32[]{:S(2)}, u32[]{:S(2)}) collective-permute-start(bf16[320,256]{1,0:T(8,128)(2,1)S(1)} %add_convert_fusion.2), channel_id=1, source_target_pairs={{0,4},{1,3},{2,6},{3,1},{4,0},{5,7},{6,2},{7,5},{8,12},{9,11},{10,... | collective-permute-start | bytes 491528 | tf_op jit(solution)/shard_map/ppermute | solution.py:515
  54.6 9.3 %collective-permute-start.13 = (bf16[320,256]{1,0:T(8,128)(2,1)S(1)}, bf16[320,256]{1,0:T(8,128)(2,1)S(1)}, u32[]{:S(2)}, u32[]{:S(2)}) collective-permute-start(bf16[320,256]{1,0:T(8,128)(2,1)S(1)} %add_convert_fusion.1), channel_id=1, source_target_pairs={{0,16},{1,9},{2,18},{3,11},{4,20},{5,13},{6,22},{7,15},{8,24},{9,1... | collective-permute-start | bytes 491528 | tf_op jit(solution)/shard_map/ppermute | solution.py:504
  56.0 8.0 %collective-permute-start.15 = (bf16[320,256]{1,0:T(8,128)(2,1)S(1)}, bf16[320,256]{1,0:T(8,128)(2,1)S(1)}, u32[]{:S(2)}, u32[]{:S(2)}) collective-permute-start(bf16[320,256]{1,0:T(8,128)(2,1)S(1)} %add_convert_fusion.1), channel_id=1, source_target_pairs={{0,24},{1,25},{2,26},{3,27},{4,28},{5,29},{6,30},{7,31},{8,16},{9,... | collective-permute-start | bytes 491528 | tf_op jit(solution)/shard_map/ppermute | solution.py:504
  60.1 5.3 %collective-permute-start.16 = (bf16[320,256]{1,0:T(8,128)(2,1)S(1)}, bf16[320,256]{1,0:T(8,128)(2,1)S(1)}, u32[]{:S(2)}, u32[]{:S(2)}) collective-permute-start(bf16[320,256]{1,0:T(8,128)(2,1)S(1)} %add_convert_fusion.1), channel_id=1, source_target_pairs={{0,8},{1,17},{2,10},{3,19},{4,12},{5,21},{6,14},{7,23},{8,0},{9,25... | collective-permute-start | bytes 491528 | tf_op jit(solution)/shard_map/ppermute | solution.py:504
  64.0 3.3 %collective-permute-start.14 = (bf16[640,256]{1,0:T(8,128)(2,1)S(1)}, bf16[640,256]{1,0:T(8,128)(2,1)S(1)}, u32[]{:S(2)}, u32[]{:S(2)}) collective-permute-start(bf16[640,256]{1,0:T(8,128)(2,1)S(1)} %pad_maximum_fusion.refs_0_), channel_id=1, source_target_pairs={{0,1},{1,0},{2,3},{3,2},{4,5},{5,4},{6,7},{7,6},{8,9},{9,8},{10,11... | collective-permute-start | bytes 983048 | tf_op jit(solution)/shard_map/ppermute | solution.py:482
  65.5 1.8 %collective-permute-start.17 = (bf16[640,256]{1,0:T(8,128)(2,1)S(1)}, bf16[640,256]{1,0:T(8,128)(2,1)S(1)}, u32[]{:S(2)}, u32[]{:S(2)}) collective-permute-start(bf16[640,256]{1,0:T(8,128)(2,1)S(1)} %constant_dynamic-update-slice_fusion.refs_1_), channel_id=1, source_target_pairs={{0,1},{1,0},{2,3},{3,2},{4,5},{5,4},{6,7},{7,6},{8,9},{9,8},{10,11... | collective-permute-start | bytes 983048 | tf_op jit(solution)/shard_map/ppermute | solution.py:482

commit v3 on v1

--- a/solution.py
+++ b/solution.py
@@ -391,26 +391,30 @@
     return pl.ds(pl.multiple_of((place_ref[0] ^ partner) * size, TILE), size)
 
 
-def pair_kernel(place_ref, one_ref, other_ref, *out_refs):
-    members = len(out_refs)
+def pair_kernel(members, place_ref, one_ref, other_ref, *rest):
+    out_refs = rest[-members:]
+    rows = one_ref.shape[0] // members
     for k, out_ref in enumerate(out_refs):
         here = share_rows(one_ref.shape[0], members, place_ref, place_ref[1], k)
         total = one_ref[here, :].astype(F32) + other_ref[here, :].astype(F32)
-        out_ref[...] = total.astype(BF16)
-
-
-def pair_sums(place, one, other, members):
+        out_ref[:rows, :] = total.astype(BF16)
+    for beside_ref in rest[:-members]:
+        out_refs[1][rows:, :] = beside_ref[...]
+
+
+def pair_sums(place, one, other, members, beside):
     rows, wide = one.shape
     share = jax.ShapeDtypeStruct((rows // members, wide), BF16)
-    return pl.pallas_call(
-        pair_kernel,
-        in_specs=[scalars()] + [whole()] * 2,
+    first = jax.ShapeDtypeStruct((rows // members + sum(x.shape[0] for x in beside), wide), BF16)
+    return pl.pallas_call(
+        functools.partial(pair_kernel, members),
+        in_specs=[scalars()] + [whole()] * (2 + len(beside)),
         out_specs=[whole()] * members,
-        out_shape=[share] * members,
+        out_shape=[share, first] + [share] * (members - 2),
         compiler_params=params(16),
         cost_estimate=cost(0, 6 * rows * wide),
         name="pair_sums",
-    )(place, one, other)
+    )(place, one, other, *beside)
 
 
 def laid_turns(members):
@@ -488,7 +492,11 @@
 
 
 def sum_over_slice(shares, two):
-    own = jnp.concatenate([added(*trade(shares)), two], axis=0)
+    got = trade(shares)
+    rows = shares[0].shape[0]
+    if got[1].shape[0] > rows:
+        two = added(two, got[1][rows:])
+    own = jnp.concatenate([added(*[array[:rows] for array in got]), two], axis=0)
     n_copy = lax.axis_size("copy")
     steps = [2 << bit for bit in range((n_copy // 2).bit_length() - 1)]
     for near, far in zip(steps, reversed(steps)):
@@ -505,13 +513,12 @@
     if members != 4 or rows != middle:
         feats = [own] + [exchange(own, "clique", k) for k in range(1, members)]
         got = shares[:1] + [exchange(shares[k], "clique", k) for k in range(1, members)]
-        return feats, added(*got)
+        return feats, added(*got), []
     one, other = exchange(own, "clique", 1), exchange(own, "clique", 2)
     top = exchange(jnp.concatenate([other[:middle], shares[1]], axis=1), "clique", 1)
     bottom = exchange(jnp.concatenate([one[middle:], shares[2]], axis=1), "clique", 2)
-    far = exchange(shares[3], "clique", 3)
-    total = added(shares[0], top[:, d_in:], bottom[:, d_in:], far)
-    return [own, one, other, top, bottom], total
+    total = added(shares[0], top[:, d_in:], bottom[:, d_in:])
+    return [own, one, other, top, bottom], total, shares[3:]
 
 
 def on_device(
@@ -530,12 +537,12 @@
         place, batch_count, out_grad, pre_act, layer_two, hot_slots.T, shard_rows * n_clique, shard_rows
     )
     two = added(own_two, exchange(twin_two, "copy", 1))
-    feats, two = gather(half_feats, two)
+    feats, two, far = gather(half_feats, two)
     send, keep, words = hot_sums(words, row_grad, cold_index.T, cold_rows, fanout)
     other = exchange(send, "copy", 1)
     cold = cold_grad(words, cold_index.T, row_grad, cold_feats, fanout)
     own_one, twin_one = join(place, cold, keep, other, feats)
-    shares = pair_sums(place, own_one, exchange(twin_one, "copy", 1), n_clique)
+    shares = pair_sums(place, own_one, exchange(twin_one, "copy", 1), n_clique, far)
     shares = sum_over_slice(shares, two)
     middle = n_clique // 2
     shares = [shares[turn] for turn in laid_turns(n_clique)]

time: 68.2 us -> 69.2 us (1.015)
  waiting for transfers between devices: 19.3 us -> 22.8 us
  starting transfers between devices: 20.3 us -> 17.4 us
    ppermute x10 -> x9, starting transfers between devices: 9.52 us -> 6.68 us  [exchange(): lax.ppermute(array, axis, [(source, source ^ step) for source in range(si...]
    ppermute x10 -> x9, waiting for transfers between devices: 0.03 us -> 1.73 us  [exchange(): lax.ppermute(array, axis, [(source, source ^ step) for source in range(si...]
    ppermute x6, waiting for transfers between devices: 9.77 us -> 11 us  [trade(): lax.ppermute(arrays[turn], ('clique', 'copy'), route_of(n_clique, n_copy,...]
  transfers between devices with their start and end apart: 18 -> 17, of which waited for: 7 -> 8; matrix products, arithmetic and copies ran while one was open for 0% -> 0% of each run, Pallas kernels for 31% -> 30%
where the time goes in v3:
time: 69.2 us; the launch traced here: 68.5 us
  Pallas kernels  25 us (36%)
  waiting for transfers between devices  22.8 us (33%)
  starting transfers between devices  17.4 us (25%)
  between operations  1.72 us (2%)
  local copies, waits for them, and re-layouts  1.23 us (2%)
    ppermute x6, waiting for transfers between devices, trade(): lax.ppermute(arrays[turn], ('clique', 'copy'), route_of(n_clique, n_copy,...  11 us
    ppermute x2, waiting for transfers between devices, sum_over_slice(): own = added(own, lax.ppermute(own, 'copy', route))  10.1 us
    pallas_call x1, Pallas kernels, cold_grad(): pl.pallas_call(functools.partial(cold_kernel, 1.0 / fanout), in_specs=[wh...  7.97 us
    ppermute x6, starting transfers between devices, trade(): lax.ppermute(arrays[turn], ('clique', 'copy'), route_of(n_clique, n_copy,...  7.11 us
    ppermute x9, starting transfers between devices, exchange(): lax.ppermute(array, axis, [(source, source ^ step) for source in range(si...  6.68 us
    pallas_call x1, Pallas kernels, hot_sums(): pl.pallas_call(functools.partial(hot_kernel, 1.0 / fanout), in_specs=[who...  5.92 us
    pallas_call x1, Pallas kernels, row_gradients(): pl.pallas_call(functools.partial(rows_kernel, shard_rows.bit_length() - 1...  4.88 us
    ppermute x2, starting transfers between devices, sum_over_slice(): own = added(own, lax.ppermute(own, 'copy', route))  3.57 us
  transfers between devices with their start and end apart: 17, of which 8 were waited for; matrix products, arithmetic and copies ran while one was open for 0% of the time, Pallas kernels for 30%

profile of v3, /device:TPU:0, one launch (start us, length us, event | category | flops | bytes accessed | tf_op | source)
XLA Modules:
  0.0 68.5 jit_solution(10416434812158194856)
XLA Ops:
  0.6 0.1 pad_add_fusion.place_ref
  0.7 1.1 %copy-done.3 = bf16[512,768]{1,0:T(8,128)(2,1)S(1)} copy-done((bf16[512,768]{1,0:T(8,128)(2,1)S(1)}, bf16[512,768]{1,0:T(8,128)(2,1)}, u32[]{:S(2)}) %copy-start.3) | copy-done | bytes 786456
  1.9 0.6 half_of.1.rest_0_
  2.4 3.0 %collective-permute-start.2 = (bf16[256,768]{1,0:T(8,128)(2,1)S(1)}, bf16[256,768]{1,0:T(8,128)(2,1)S(1)}, u32[]{:S(2)}, u32[]{:S(2)}) collective-permute-start(bf16[256,768]{1,0:T(8,128)(2,1)S(1)} %half_of.1.rest_0_), channel_id=1, source_target_pairs={{0,16},{8,24},{16,0},{24,8},{1,17},{9,25},{17,1},{25,9},{2,18},{10... | collective-permute-start | bytes 1179656 | tf_op jit(solution)/shard_map/ppermute | solution.py:467
  5.5 1.5 %collective-permute-start.1 = (bf16[256,768]{1,0:T(8,128)(2,1)S(1)}, bf16[256,768]{1,0:T(8,128)(2,1)S(1)}, u32[]{:S(2)}, u32[]{:S(2)}) collective-permute-start(bf16[256,768]{1,0:T(8,128)(2,1)S(1)} %half_of.1.rest_0_), channel_id=1, source_target_pairs={{0,8},{8,0},{16,24},{24,16},{1,9},{9,1},{17,25},{25,17},{2,10},{10... | collective-permute-start | bytes 1179656 | tf_op jit(solution)/shard_map/ppermute | solution.py:467
  7.7 0.0 copy-start.6
  7.7 4.9 %row_gradients.1 = (bf16[2048,512]{1,0:T(8,128)(2,1)S(1)}, bf16[512,256]{1,0:T(8,128)(2,1)S(1)}, bf16[512,256]{1,0:T(8,128)(2,1)S(1)}, s16[32,16,2048]{2,1,0:T(8,128)(2,1)S(1)}) custom-call(s32[2]{0:T(128)S(1)} %pad_add_fusion.place_ref, s32[1]{0:T(128)S(6)} %copy.15.count_ref, s32[10,2048]{1,0:T(8,128)S(1)} %bitcast.4, bf16[2048,512]{1,0:T(8,128)(2,1)S(1)} %copy-done.1, ...), custom_call_target="tpu_custom_call" | custom-call | flops 10000000000 | bytes 100000000 | tf_op jit(solution)/shard_map/row_gradients/pallas_call | solution.py:178
  12.6 0.1 collective-permute-start.3
  12.6 0.0 copy-start
  12.7 5.9 %hot_sums.1 = (bf16[1024,512]{1,0:T(8,128)(2,1)S(1)}, bf16[1024,512]{1,0:T(8,128)(2,1)S(1)}, s16[32,16,1024]{2,1,0:T(8,128)(2,1)S(1)}) custom-call(s16[32,16,2048]{2,1,0:T(8,128)(2,1)S(1)} %get-tuple-element.17.word_in, bf16[2048,512]{1,0:T(8,128)(2,1)S(1)} %get-tuple-element.18.row_grad_in, s32[15,2048]{1,0:T(8,128)S(1)} %bitcast.5), custom_call_target="tpu_custom_call" | custom-call | flops 10000000000 | bytes 100000000 | tf_op jit(solution)/shard_map/hot_sums/pallas_call | solution.py:241
  18.6 0.5 collective-permute-start
  19.1 0.0 collective-permute-done.3
  19.1 0.1 add_convert_fusion
  19.2 0.0 collective-permute-done.2.rest_2_
  19.3 0.5 collective-permute-start.4
  19.8 0.0 collective-permute-done.1.rest_1_
  19.9 0.5 collective-permute-start.5
  20.3 8.0 %cold_grad.1.cold_ref = f32[768,512]{1,0:T(8,128)S(1)} custom-call(s16[32,16,1024]{2,1,0:T(8,128)(2,1)S(1)} %get-tuple-element.19.word_in, s32[15,2048]{1,0:T(8,128)S(1)} %bitcast.6, bf16[2048,512]{1,0:T(8,128)(2,1)S(1)} %get-tuple-element.18.row_grad_in, bf16[2048,768]{1,0:T(8,128)(2,1)S(1)} %copy-done), custom_call_target="tpu_custom_call" | custom-call | flops 10000000000 | bytes 100000000 | tf_op jit(solution)/shard_map/cold_grad/pallas_call | solution.py:310
  28.3 0.0 collective-permute-done.4.rest_3_
  28.3 0.0 collective-permute-done.5.rest_4_
  28.3 0.0 collective-permute-done.other_ref
  28.4 1.6 %join.1 = (bf16[768,256]{1,0:T(8,128)(2,1)S(1)}, bf16[768,256]{1,0:T(8,128)(2,1)S(1)}) custom-call(s32[2]{0:T(128)S(1)} %pad_add_fusion.place_ref, f32[768,512]{1,0:T(8,128)S(1)} %cold_grad.1.cold_ref, bf16[1024,512]{1,0:T(8,128)(2,1)S(1)} %get-tuple-element.20.keep_ref, bf16[1024,512]{1,0:T(8,128)(2,1)S(1)} %collective-permute-done.other_ref, ...), custom_call_target="tpu_custom_call" | custom-call | flops 805306368 | bytes 1572864 | tf_op jit(solution)/shard_map/join/pallas_call | solution.py:368
  30.0 0.1 collective-permute-start.6
  30.1 1.7 %collective-permute-done.6.other_ref = bf16[768,256]{1,0:T(8,128)(2,1)S(1)} collective-permute-done((bf16[768,256]{1,0:T(8,128)(2,1)S(1)}, bf16[768,256]{1,0:T(8,128)(2,1)S(1)}, u32[]{:S(2)}, u32[]{:S(2)}) %collective-permute-start.6) | collective-permute-done | bytes 393248 | tf_op jit(solution)/shard_map/ppermute | solution.py:467
  31.8 0.6 pair_sums.1
  32.4 2.7 %collective-permute-start.7 = (bf16[320,256]{1,0:T(8,128)(2,1)S(1)}, bf16[320,256]{1,0:T(8,128)(2,1)S(1)}, u32[]{:S(2)}, u32[]{:S(2)}) collective-permute-start(bf16[320,256]{1,0:T(8,128)(2,1)S(1)} %get-tuple-element.27), channel_id=1, source_target_pairs={{0,24},{1,25},{2,26},{3,27},{4,28},{5,29},{6,30},{7,31},{8,16},{9,... | collective-permute-start | bytes 491528 | tf_op jit(solution)/shard_map/ppermute | solution.py:489
  35.1 0.5 collective-permute-start.8
  35.6 0.4 collective-permute-start.9
  36.0 4.5 %collective-permute-done.7 = bf16[320,256]{1,0:T(8,128)(2,1)S(1)} collective-permute-done((bf16[320,256]{1,0:T(8,128)(2,1)S(1)}, bf16[320,256]{1,0:T(8,128)(2,1)S(1)}, u32[]{:S(2)}, u32[]{:S(2)}) %collective-permute-start.7) | collective-permute-done | bytes 163872 | tf_op jit(solution)/shard_map/ppermute | solution.py:489
  40.5 1.5 %collective-permute-done.8 = bf16[192,256]{1,0:T(8,128)(2,1)S(1)} collective-permute-done((bf16[192,256]{1,0:T(8,128)(2,1)S(1)}, bf16[192,256]{1,0:T(8,128)(2,1)S(1)}, u32[]{:S(2)}, u32[]{:S(2)}) %collective-permute-start.8) | collective-permute-done | bytes 98336 | tf_op jit(solution)/shard_map/ppermute | solution.py:489
  41.9 0.0 collective-permute-done.9
  41.9 0.1 add_convert_fusion.3
  42.0 1.6 %collective-permute-start.10 = (bf16[320,256]{1,0:T(8,128)(2,1)S(1)}, bf16[320,256]{1,0:T(8,128)(2,1)S(1)}, u32[]{:S(2)}, u32[]{:S(2)}) collective-permute-start(bf16[320,256]{1,0:T(8,128)(2,1)S(1)} %pad_maximum_fusion.3), channel_id=1, source_target_pairs={{0,2},{1,5},{2,0},{3,7},{4,6},{5,1},{6,4},{7,3},{8,10},{9,13},{10,... | collective-permute-start | bytes 491528 | tf_op jit(solution)/shard_map/ppermute | solution.py:504
  43.7 5.2 %collective-permute-done.10 = bf16[320,256]{1,0:T(8,128)(2,1)S(1)} collective-permute-done((bf16[320,256]{1,0:T(8,128)(2,1)S(1)}, bf16[320,256]{1,0:T(8,128)(2,1)S(1)}, u32[]{:S(2)}, u32[]{:S(2)}) %collective-permute-start.10) | collective-permute-done | bytes 163872 | tf_op jit(solution)/shard_map/ppermute | solution.py:504
  48.9 1.9 %collective-permute-start.11 = (bf16[320,256]{1,0:T(8,128)(2,1)S(1)}, bf16[320,256]{1,0:T(8,128)(2,1)S(1)}, u32[]{:S(2)}, u32[]{:S(2)}) collective-permute-start(bf16[320,256]{1,0:T(8,128)(2,1)S(1)} %add_convert_fusion.2), channel_id=1, source_target_pairs={{0,4},{1,3},{2,6},{3,1},{4,0},{5,7},{6,2},{7,5},{8,12},{9,11},{10,... | collective-permute-start | bytes 491528 | tf_op jit(solution)/shard_map/ppermute | solution.py:504
  50.9 4.8 %collective-permute-done.11 = bf16[320,256]{1,0:T(8,128)(2,1)S(1)} collective-permute-done((bf16[320,256]{1,0:T(8,128)(2,1)S(1)}, bf16[320,256]{1,0:T(8,128)(2,1)S(1)}, u32[]{:S(2)}, u32[]{:S(2)}) %collective-permute-start.11) | collective-permute-done | bytes 163872 | tf_op jit(solution)/shard_map/ppermute | solution.py:504
  55.8 0.2 collective-permute-start.14
  56.0 3.2 %collective-permute-start.15 = (bf16[320,256]{1,0:T(8,128)(2,1)S(1)}, bf16[320,256]{1,0:T(8,128)(2,1)S(1)}, u32[]{:S(2)}, u32[]{:S(2)}) collective-permute-start(bf16[320,256]{1,0:T(8,128)(2,1)S(1)} %add_convert_fusion.1), channel_id=1, source_target_pairs={{0,8},{1,17},{2,10},{3,19},{4,12},{5,21},{6,14},{7,23},{8,0},{9,25... | collective-permute-start | bytes 491528 | tf_op jit(solution)/shard_map/ppermute | solution.py:489
  59.2 0.1 collective-permute-start.12
  59.3 2.7 %collective-permute-done.14 = bf16[320,256]{1,0:T(8,128)(2,1)S(1)} collective-permute-done((bf16[320,256]{1,0:T(8,128)(2,1)S(1)}, bf16[320,256]{1,0:T(8,128)(2,1)S(1)}, u32[]{:S(2)}, u32[]{:S(2)}) %collective-permute-start.14) | collective-permute-done | bytes 163872 | tf_op jit(solution)/shard_map/ppermute | solution.py:489
  62.1 2.2 %collective-permute-done.15 = bf16[320,256]{1,0:T(8,128)(2,1)S(1)} collective-permute-done((bf16[320,256]{1,0:T(8,128)(2,1)S(1)}, bf16[320,256]{1,0:T(8,128)(2,1)S(1)}, u32[]{:S(2)}, u32[]{:S(2)}) %collective-permute-start.15) | collective-permute-done | bytes 163872 | tf_op jit(solution)/shard_map/ppermute | solution.py:489
  64.3 0.1 collective-permute-start.16
  64.3 0.2 collective-permute-done.12
  64.5 0.4 collective-permute-start.13
  64.9 1.7 %lay.2 = (f32[768,512]{1,0:T(8,128)}, f32[512,512]{1,0:T(8,128)}) custom-call(s32[2]{0:T(128)S(1)} %pad_add_fusion.place_ref, bf16[640,256]{1,0:T(8,128)(2,1)S(1)} %pad_maximum_fusion.refs_0_, bf16[640,256]{1,0:T(8,128)(2,1)S(1)} %constant_dynamic-update-slice_fusion.refs_1_), custom_call_target="tpu_custom_call" | custom-call | flops 10000000000 | bytes 100000000 | tf_op jit(solution)/shard_map/lay/pallas_call | solution.py:451
  66.6 0.0 collective-permute-done.16.refs_1_
  66.6 0.0 collective-permute-done.13.refs_0_
  66.6 1.7 %lay.3 = (f32[768,512]{1,0:T(8,128)}, f32[512,512]{1,0:T(8,128)}) custom-call(s32[2]{0:T(128)S(1)} %pad_add_fusion.place_ref, bf16[640,256]{1,0:T(8,128)(2,1)S(1)} %collective-permute-done.13.refs_0_, bf16[640,256]{1,0:T(8,128)(2,1)S(1)} %collective-permute-done.16.refs_1_, ...), custom_call_target="tpu_custom_call", output_to_operand_aliasing={{0}: (3, {}), {1}: (4, {})} | custom-call | flops 10000000000 | bytes 100000000 | tf_op jit(solution)/shard_map/lay/pallas_call | solution.py:451
  (23 shorter events, 0.3 us)
Async XLA Ops:
  0.7 1.1 %copy-start.3 = (bf16[512,768]{1,0:T(8,128)(2,1)S(1)}, bf16[512,768]{1,0:T(8,128)(2,1)}, u32[]{:S(2)}) copy-start(bf16[512,768]{1,0:T(8,128)(2,1)} %feats_ref.3) | copy-start | bytes 2359300
  1.8 5.8 %copy-start.1 = (bf16[2048,512]{1,0:T(8,128)(2,1)S(1)}, bf16[2048,512]{1,0:T(8,128)(2,1)}, u32[]{:S(2)}) copy-start(bf16[2048,512]{1,0:T(8,128)(2,1)} %out_grad_ref.1) | copy-start | bytes 6291460
  1.8 5.8 %copy-start.2 = (bf16[2048,512]{1,0:T(8,128)(2,1)S(1)}, bf16[2048,512]{1,0:T(8,128)(2,1)}, u32[]{:S(2)}) copy-start(bf16[2048,512]{1,0:T(8,128)(2,1)} %pre_act_ref.1) | copy-start | bytes 6291460
  1.8 5.8 %copy-start.4 = (bf16[512,512]{1,0:T(8,128)(2,1)S(1)}, bf16[512,512]{1,0:T(8,128)(2,1)}, u32[]{:S(2)}) copy-start(bf16[512,512]{1,0:T(8,128)(2,1)} %layer_two_ref.1) | copy-start | bytes 1572868
  1.9 5.8 %copy-start.5 = (s32[2048,10]{0,1:T(8,128)S(1)}, s32[2048,10]{0,1:T(8,128)}, u32[]{:S(2)}) copy-start(s32[2048,10]{0,1:T(8,128)} %param.12) | copy-start | bytes 245764
  2.4 16.8 %collective-permute-start.2 = (bf16[256,768]{1,0:T(8,128)(2,1)S(1)}, bf16[256,768]{1,0:T(8,128)(2,1)S(1)}, u32[]{:S(2)}, u32[]{:S(2)}) collective-permute-start(bf16[256,768]{1,0:T(8,128)(2,1)S(1)} %half_of.1.rest_0_), channel_id=1, source_target_pairs={{0,16},{8,24},{16,0},{24,8},{1,17},{9,25},{17,1},{25,9},{2,18},{10... | collective-permute-start | bytes 1179656 | tf_op jit(solution)/shard_map/ppermute | solution.py:467
  5.5 14.3 %collective-permute-start.1 = (bf16[256,768]{1,0:T(8,128)(2,1)S(1)}, bf16[256,768]{1,0:T(8,128)(2,1)S(1)}, u32[]{:S(2)}, u32[]{:S(2)}) collective-permute-start(bf16[256,768]{1,0:T(8,128)(2,1)S(1)} %half_of.1.rest_0_), channel_id=1, source_target_pairs={{0,8},{8,0},{16,24},{24,16},{1,9},{9,1},{17,25},{25,17},{2,10},{10... | collective-permute-start | bytes 1179656 | tf_op jit(solution)/shard_map/ppermute | solution.py:467
  7.7 5.0 %copy-start.6 = (s32[2048,15]{0,1:T(8,128)S(1)}, s32[2048,15]{0,1:T(8,128)}, u32[]{:S(2)}) copy-start(s32[2048,15]{0,1:T(8,128)} %param.13) | copy-start | bytes 368644
  12.6 6.6 %collective-permute-start.3 = (bf16[512,256]{1,0:T(8,128)(2,1)S(1)}, bf16[512,256]{1,0:T(8,128)(2,1)S(1)}, u32[]{:S(2)}, u32[]{:S(2)}) collective-permute-start(bf16[512,256]{1,0:T(8,128)(2,1)S(1)} %get-tuple-element.23), channel_id=1, source_target_pairs={{0,1},{1,0},{2,3},{3,2},{4,5},{5,4},{6,7},{7,6},{8,9},{9,8},{10,11... | collective-permute-start | bytes 786440 | tf_op jit(solution)/shard_map/ppermute | solution.py:467
  12.6 7.7 %copy-start = (bf16[2048,768]{1,0:T(8,128)(2,1)S(1)}, bf16[2048,768]{1,0:T(8,128)(2,1)}, u32[]{:S(2)}) copy-start(bf16[2048,768]{1,0:T(8,128)(2,1)} %feats_ref.2) | copy-start | bytes 9437188
  18.6 9.8 %collective-permute-start = (bf16[1024,512]{1,0:T(8,128)(2,1)S(1)}, bf16[1024,512]{1,0:T(8,128)(2,1)S(1)}, u32[]{:S(2)}, u32[]{:S(2)}) collective-permute-start(bf16[1024,512]{1,0:T(8,128)(2,1)S(1)} %get-tuple-element.21), channel_id=1, source_target_pairs={{0,1},{1,0},{2,3},{3,2},{4,5},{5,4},{6,7},{7,6},{8,9},{9,8},{10,11... | collective-permute-start | bytes 3145736 | tf_op jit(solution)/shard_map/ppermute | solution.py:467
  19.3 9.0 %collective-permute-start.4 = (bf16[128,1024]{1,0:T(8,128)(2,1)S(1)}, bf16[128,1024]{1,0:T(8,128)(2,1)S(1)}, u32[]{:S(2)}, u32[]{:S(2)}) collective-permute-start(bf16[128,1024]{1,0:T(8,128)(2,1)S(1)} %pad_maximum_fusion.1), channel_id=1, source_target_pairs={{0,8},{8,0},{16,24},{24,16},{1,9},{9,1},{17,25},{25,17},{2,10},{10... | collective-permute-start | bytes 786440 | tf_op jit(solution)/shard_map/ppermute | solution.py:467
  19.9 8.5 %collective-permute-start.5 = (bf16[128,1024]{1,0:T(8,128)(2,1)S(1)}, bf16[128,1024]{1,0:T(8,128)(2,1)S(1)}, u32[]{:S(2)}, u32[]{:S(2)}) collective-permute-start(bf16[128,1024]{1,0:T(8,128)(2,1)S(1)} %pad_maximum_fusion.2), channel_id=1, source_target_pairs={{0,16},{8,24},{16,0},{24,8},{1,17},{9,25},{17,1},{25,9},{2,18},{10... | collective-permute-start | bytes 786440 | tf_op jit(solution)/shard_map/ppermute | solution.py:467
  30.0 1.8 %collective-permute-start.6 = (bf16[768,256]{1,0:T(8,128)(2,1)S(1)}, bf16[768,256]{1,0:T(8,128)(2,1)S(1)}, u32[]{:S(2)}, u32[]{:S(2)}) collective-permute-start(bf16[768,256]{1,0:T(8,128)(2,1)S(1)} %get-tuple-element.25), channel_id=1, source_target_pairs={{0,1},{1,0},{2,3},{3,2},{4,5},{5,4},{6,7},{7,6},{8,9},{9,8},{10,11... | collective-permute-start | bytes 1179656 | tf_op jit(solution)/shard_map/ppermute | solution.py:467
  32.4 8.0 %collective-permute-start.7 = (bf16[320,256]{1,0:T(8,128)(2,1)S(1)}, bf16[320,256]{1,0:T(8,128)(2,1)S(1)}, u32[]{:S(2)}, u32[]{:S(2)}) collective-permute-start(bf16[320,256]{1,0:T(8,128)(2,1)S(1)} %get-tuple-element.27), channel_id=1, source_target_pairs={{0,24},{1,25},{2,26},{3,27},{4,28},{5,29},{6,30},{7,31},{8,16},{9,... | collective-permute-start | bytes 491528 | tf_op jit(solution)/shard_map/ppermute | solution.py:489
  35.1 6.8 %collective-permute-start.8 = (bf16[192,256]{1,0:T(8,128)(2,1)S(1)}, bf16[192,256]{1,0:T(8,128)(2,1)S(1)}, u32[]{:S(2)}, u32[]{:S(2)}) collective-permute-start(bf16[192,256]{1,0:T(8,128)(2,1)S(1)} %get-tuple-element.28), channel_id=1, source_target_pairs={{0,8},{1,17},{2,10},{3,19},{4,12},{5,21},{6,14},{7,23},{8,0},{9,25... | collective-permute-start | bytes 294920 | tf_op jit(solution)/shard_map/ppermute | solution.py:489
  35.6 6.4 %collective-permute-start.9 = (bf16[192,256]{1,0:T(8,128)(2,1)S(1)}, bf16[192,256]{1,0:T(8,128)(2,1)S(1)}, u32[]{:S(2)}, u32[]{:S(2)}) collective-permute-start(bf16[192,256]{1,0:T(8,128)(2,1)S(1)} %get-tuple-element.29), channel_id=1, source_target_pairs={{0,16},{1,9},{2,18},{3,11},{4,20},{5,13},{6,22},{7,15},{8,24},{9,1... | collective-permute-start | bytes 294920 | tf_op jit(solution)/shard_map/ppermute | solution.py:489
  42.0 6.9 %collective-permute-start.10 = (bf16[320,256]{1,0:T(8,128)(2,1)S(1)}, bf16[320,256]{1,0:T(8,128)(2,1)S(1)}, u32[]{:S(2)}, u32[]{:S(2)}) collective-permute-start(bf16[320,256]{1,0:T(8,128)(2,1)S(1)} %pad_maximum_fusion.3), channel_id=1, source_target_pairs={{0,2},{1,5},{2,0},{3,7},{4,6},{5,1},{6,4},{7,3},{8,10},{9,13},{10,... | collective-permute-start | bytes 491528 | tf_op jit(solution)/shard_map/ppermute | solution.py:504
  48.9 6.8 %collective-permute-start.11 = (bf16[320,256]{1,0:T(8,128)(2,1)S(1)}, bf16[320,256]{1,0:T(8,128)(2,1)S(1)}, u32[]{:S(2)}, u32[]{:S(2)}) collective-permute-start(bf16[320,256]{1,0:T(8,128)(2,1)S(1)} %add_convert_fusion.2), channel_id=1, source_target_pairs={{0,4},{1,3},{2,6},{3,1},{4,0},{5,7},{6,2},{7,5},{8,12},{9,11},{10,... | collective-permute-start | bytes 491528 | tf_op jit(solution)/shard_map/ppermute | solution.py:504
  55.8 6.3 %collective-permute-start.14 = (bf16[320,256]{1,0:T(8,128)(2,1)S(1)}, bf16[320,256]{1,0:T(8,128)(2,1)S(1)}, u32[]{:S(2)}, u32[]{:S(2)}) collective-permute-start(bf16[320,256]{1,0:T(8,128)(2,1)S(1)} %add_convert_fusion.1), channel_id=1, source_target_pairs={{0,24},{1,25},{2,26},{3,27},{4,28},{5,29},{6,30},{7,31},{8,16},{9,... | collective-permute-start | bytes 491528 | tf_op jit(solution)/shard_map/ppermute | solution.py:489
  56.0 8.3 %collective-permute-start.15 = (bf16[320,256]{1,0:T(8,128)(2,1)S(1)}, bf16[320,256]{1,0:T(8,128)(2,1)S(1)}, u32[]{:S(2)}, u32[]{:S(2)}) collective-permute-start(bf16[320,256]{1,0:T(8,128)(2,1)S(1)} %add_convert_fusion.1), channel_id=1, source_target_pairs={{0,8},{1,17},{2,10},{3,19},{4,12},{5,21},{6,14},{7,23},{8,0},{9,25... | collective-permute-start | bytes 491528 | tf_op jit(solution)/shard_map/ppermute | solution.py:489
  59.2 5.3 %collective-permute-start.12 = (bf16[320,256]{1,0:T(8,128)(2,1)S(1)}, bf16[320,256]{1,0:T(8,128)(2,1)S(1)}, u32[]{:S(2)}, u32[]{:S(2)}) collective-permute-start(bf16[320,256]{1,0:T(8,128)(2,1)S(1)} %add_convert_fusion.1), channel_id=1, source_target_pairs={{0,16},{1,9},{2,18},{3,11},{4,20},{5,13},{6,22},{7,15},{8,24},{9,1... | collective-permute-start | bytes 491528 | tf_op jit(solution)/shard_map/ppermute | solution.py:489
  64.3 2.3 %collective-permute-start.16 = (bf16[640,256]{1,0:T(8,128)(2,1)S(1)}, bf16[640,256]{1,0:T(8,128)(2,1)S(1)}, u32[]{:S(2)}, u32[]{:S(2)}) collective-permute-start(bf16[640,256]{1,0:T(8,128)(2,1)S(1)} %constant_dynamic-update-slice_fusion.refs_1_), channel_id=1, source_target_pairs={{0,1},{1,0},{2,3},{3,2},{4,5},{5,4},{6,7},{7,6},{8,9},{9,8},{10,11... | collective-permute-start | bytes 983048 | tf_op jit(solution)/shard_map/ppermute | solution.py:467
  64.5 2.1 %collective-permute-start.13 = (bf16[640,256]{1,0:T(8,128)(2,1)S(1)}, bf16[640,256]{1,0:T(8,128)(2,1)S(1)}, u32[]{:S(2)}, u32[]{:S(2)}) collective-permute-start(bf16[640,256]{1,0:T(8,128)(2,1)S(1)} %pad_maximum_fusion.refs_0_), channel_id=1, source_target_pairs={{0,1},{1,0},{2,3},{3,2},{4,5},{5,4},{6,7},{7,6},{8,9},{9,8},{10,11... | collective-permute-start | bytes 983048 | tf_op jit(solution)/shard_map/ppermute | solution.py:467
